TPU v7x, 128 devices: a whole 4x4x4 slice. The times are simulated.
128 devices in a mesh: obs: 16 (over y, z), emis: 8 (over x, core).
Axes of the slice: x: 4, y: 4, z: 4, core: 2. Of those that a mesh axis runs over, the one named last changes fastest.
Arguments:
- control: float32 [2048, 256, 128], P(('obs', 'emis')), may hold values from -6 to 6
- prior_flux: float32 [2048, 256], P(('obs', 'emis')), may hold values from 0.1 to 3
- correlation: float32 [256, 256], replicated, may hold values from -0.375 to 0.375
- footprints: bfloat16 [512, 24, 256, 256], P(('obs', 'emis')), may hold values from -0.078125 to 0.078125
- obs_values: float32 [131072, 128], P(('obs', 'emis')), may hold values from -6 to 6
- obs_weights: float32 [131072], P(('obs', 'emis')), may hold values from 0.2 to 5
- tile_ids: int32 [512, 24], P(('obs', 'emis')), may hold values from 0 to 2047, as said below
Outputs:
- gradient: float32 [2048, 256, 128], P(('obs', 'emis'))
Inputs may be any that keep to these rules, and one draw needn't show every extreme that they name: `tile_ids`: tile t is owned by the device of index t // 16, counting obs slowest. The 96 tiles touched by the blocks of one device are all distinct and name each owner device at most 1 times; one owner, the same for every device, is named exactly 1 times by every device.
All inputs are finite; a program needn't handle non-finite values.
Results may differ from a plain program's by a relative error of at most 0.0041.
Values may be sent and summed in bfloat16 or wider, within the bound.
A program may use at most 128 MiB of HBM per device.

v0:
```python
import jax
import jax.numpy as jnp
from jax import lax
from jax.sharding import PartitionSpec as P


def route_tiles(payload):
    return lax.all_to_all(payload, ("obs", "emis"), split_axis=0, concat_axis=0, tiled=True)


def route_partials(payload):
    return lax.all_to_all(payload, ("obs", "emis"), split_axis=0, concat_axis=0, tiled=True)


def per_device(control, prior_flux, correlation, footprints, obs_values, obs_weights, tile_ids):
    owners = lax.axis_size(("obs", "emis"))
    tile_dev, cells, members = control.shape
    blocks, touched = tile_ids.shape
    per_block = footprints.shape[2]
    request_count = blocks * touched
    capacity = max(1, -(-request_count // owners))
    slot_count = owners * capacity
    emission = prior_flux[:, :, None] + jnp.einsum(
        "ct,ntm->ncm", correlation, control, precision=lax.Precision.HIGHEST
    )
    emission_bf = emission.astype(jnp.bfloat16)
    flat_ids = tile_ids.reshape(-1)
    owner_of = flat_ids // tile_dev
    local_tile = flat_ids % tile_dev
    order = jnp.arange(request_count, dtype=jnp.int32)
    earlier = (owner_of[:, None] == owner_of[None, :]) & (order[None, :] < order[:, None])
    slot_index = owner_of * capacity + jnp.sum(earlier, axis=1)
    slot_match = slot_index[:, None] == jnp.arange(slot_count, dtype=jnp.int32)[None, :]
    wanted = jnp.sum(jnp.where(slot_match, local_tile[:, None], 0), axis=0)
    in_use = jnp.sum(slot_match.astype(jnp.int32), axis=0)
    got_tile, got_use = (
        lax.all_to_all(
            wanted.reshape(owners, capacity),
            ("obs", "emis"),
            split_axis=0,
            concat_axis=0,
            tiled=True,
        ),
        lax.all_to_all(
            in_use.reshape(owners, capacity),
            ("obs", "emis"),
            split_axis=0,
            concat_axis=0,
            tiled=True,
        ),
    )
    got_tile = got_tile.reshape(-1)
    got_use = got_use.reshape(-1)
    picked = emission_bf[got_tile] * got_use[:, None, None].astype(jnp.bfloat16)
    arrived = route_tiles(picked.reshape(owners, capacity, cells, members))
    gathered = arrived.reshape(slot_count, cells, members)[slot_index].reshape(
        blocks, touched, cells, members
    )
    modeled = jnp.einsum("bkot,bktm->bom", footprints, gathered, preferred_element_type=jnp.float32)
    observed = obs_values.reshape(blocks, per_block, members)
    weights = obs_weights.reshape(blocks, per_block)
    mismatch = ((modeled - observed) * weights[:, :, None]).astype(jnp.bfloat16)
    partial_value = jnp.einsum(
        "bkot,bom->bktm", footprints, mismatch, preferred_element_type=jnp.float32
    ).astype(jnp.bfloat16)
    outgoing = (
        jnp.zeros((slot_count, cells, members), jnp.bfloat16)
        .at[slot_index]
        .set(partial_value.reshape(request_count, cells, members))
    )
    returned = route_partials(outgoing.reshape(owners, capacity, cells, members))
    selector = (
        (got_tile[None, :] == jnp.arange(tile_dev, dtype=jnp.int32)[:, None])
        & (got_use[None, :] > 0)
    ).astype(jnp.bfloat16)
    adjoint = jnp.einsum(
        "ts,scm->tcm",
        selector,
        returned.reshape(slot_count, cells, members),
        preferred_element_type=jnp.float32,
    )
    gradient = control + jnp.einsum(
        "ct,ncm->ntm", correlation, adjoint, precision=lax.Precision.HIGHEST
    )
    return gradient


def solution(mesh):
    return jax.shard_map(
        per_device,
        mesh=mesh,
        in_specs=(
            P(("obs", "emis"), None, None),
            P(("obs", "emis"), None),
            P(),
            P(("obs", "emis"), None, None, None),
            P(("obs", "emis"), None),
            P(("obs", "emis")),
            P(("obs", "emis"), None),
        ),
        out_specs=P(("obs", "emis"), None, None),
        check_vma=False,
    )
```

profile of v0, /device:TPU:1, one launch (start us, length us, event | category | flops | bytes accessed | tf_op | source)
XLA Modules:
  0.0 345.3 jit_solution(16881851608422021441)
XLA Ops:
  0.0 0.0 copy-start
  0.0 0.8 reshape.240
  0.8 0.2 convert_reduce_fusion.2
  1.0 0.1 convert_reduce_fusion.1
  1.1 0.7 copy.38
  1.9 11.5 %all-to-all-start = ((s32[128,1,1]{2,1,0:T(1,128)}), s32[128,1,1]{2,1,0:T(1,128)S(1)}, u32[]{:S(2)}, u32[]{:S(2)}) async-start(s32[128,1,1]{2,1,0:T(1,128)} %copy.38), calls=%async_computation | async-start | bytes 131072 | tf_op jit(solution)/shard_map/all_to_all | solution.py:37
  13.4 0.0 copy-done
  13.4 5.0 %fusion.8 = bf16[16,256,128]{1,2,0:T(8,128)(2,1)S(1)} fusion(f32[16,256,128]{2,1,0:T(8,128)} %param.7, f32[16,256]{1,0:T(8,128)} %param.8, f32[256,256]{1,0:T(8,128)S(1)} %copy-done), kind=kOutput, calls=%fused_computation.13 | convolution fusion | flops 1611661312 | bytes 3424256 | tf_op jit(solution)/shard_map/ct,ntm->ncm/dot_general | solution.py:23
  18.4 0.7 copy.39
  19.2 3.6 %all-to-all-done = s32[128,1,1]{2,1,0:T(1,128)S(1)} async-done(((s32[128,1,1]{2,1,0:T(1,128)}), s32[128,1,1]{2,1,0:T(1,128)S(1)}, u32[]{:S(2)}, u32[]{:S(2)}) %all-to-all-start) | async-done | bytes 544 | tf_op jit(solution)/shard_map/all_to_all | solution.py:37
  22.8 6.1 %all-to-all-start.1 = ((s32[128,1,1]{2,1,0:T(1,128)}), s32[128,1,1]{2,1,0:T(1,128)S(1)}, u32[]{:S(2)}, u32[]{:S(2)}) async-start(s32[128,1,1]{2,1,0:T(1,128)} %copy.39), calls=%async_computation.1 | async-start | bytes 131072 | tf_op jit(solution)/shard_map/all_to_all | solution.py:44
  28.9 2.4 reduce
  31.3 6.5 %gather_fusion = bf16[128,256,128]{1,2,0:T(8,128)(2,1)} fusion(bf16[16,256,128]{1,2,0:T(8,128)(2,1)S(1)} %fusion.8, s32[1024]{0:T(1024)S(1)} %pad_clamp_fusion.1), kind=kCustom, calls=%fused_computation | custom fusion | bytes 16777728 | tf_op jit(solution)/shard_map/gather | solution.py:54
  37.8 0.6 all-to-all-done.1
  38.4 1.0 convert_reduce_fusion
  39.5 7.2 %fusion.2 = bf16[128,1,256,128]{2,3,1,0:T(8,128)(2,1)} fusion(bf16[128,256,128]{1,2,0:T(8,128)(2,1)} %gather_fusion, bf16[128]{0:T(256)(128)(2,1)S(1)} %convert_reduce_fusion), kind=kLoop, calls=%fused_computation.6 | loop fusion | flops 4194304 | bytes 16777472 | tf_op jit(solution)/shard_map/mul | solution.py:54
  46.7 0.0 copy-start.2
  46.7 0.0 copy-start.1
  46.7 0.0 copy-start.3
  46.7 9.6 %all-to-all-start.2 = ((bf16[128,1,256,128]{2,3,1,0:T(8,128)(2,1)}), bf16[128,1,256,128]{2,3,1,0:T(8,128)(2,1)}, u32[]{:S(2)}, u32[]{:S(2)}) async-start(bf16[128,1,256,128]{2,3,1,0:T(8,128)(2,1)} %fusion.2), calls=%async_computation.2 | async-start | bytes 16777216 | tf_op jit(solution)/shard_map/all_to_all | solution.py:8
  56.4 0.0 copy-done.2
  56.4 0.1 reshape.241
  56.5 0.0 copy-done.1
  56.5 0.2 copy.42
  56.7 0.0 copy-done.3
  56.7 99.8 %all-to-all-done.2 = bf16[128,1,256,128]{2,3,1,0:T(8,128)(2,1)} async-done(((bf16[128,1,256,128]{2,3,1,0:T(8,128)(2,1)}), bf16[128,1,256,128]{2,3,1,0:T(8,128)(2,1)}, u32[]{:S(2)}, u32[]{:S(2)}) %all-to-all-start.2) | async-done | bytes 8388640 | tf_op jit(solution)/shard_map/all_to_all | solution.py:8
  156.5 9.4 %gather_fusion.1 = bf16[96,256,128]{1,2,0:T(8,128)(2,1)} fusion(bf16[128,256,128]{1,2,0:T(8,128)(2,1)} %bitcast.10, s32[1024]{0:T(1024)S(1)} %pad_clamp_fusion), kind=kCustom, calls=%fused_computation.1 | custom fusion | bytes 12583296 | tf_op jit(solution)/shard_map/gather | solution.py:56
  166.0 17.7 %convolution_convert_fusion = bf16[4,128,24,256]{3,1,2,0:T(8,128)(2,1)} fusion(bf16[4,24,256,256]{3,2,1,0:T(8,128)(2,1)} %param.10, f32[4,256,128]{1,2,0:T(8,128)S(1)} %copy.42, bf16[4,24,256,128]{2,3,1,0:T(8,128)(2,1)} %bitcast.68, f32[4,256]{1,0:T(4,128)S(1)} %mul.30), kind=kOutput, calls=%fused_computation.8 | convolution fusion | flops 3224764416 | bytes 25694208 | tf_op jit(solution)/shard_map/bkot,bom->bktm/dot_general | solution.py:63
  183.7 8.6 %copy.43 = bf16[96,256,128]{2,1,0:T(8,128)(2,1)} copy(bf16[96,256,128]{1,2,0:T(8,128)(2,1)} %bitcast.69) | data formatting | bytes 12582912 | tf_op jit(solution)/shard_map/reshape | solution.py:69
  192.3 5.3 %broadcast_in_dim.12 = bf16[128,256,128]{2,1,0:T(8,128)(2,1)} broadcast(bf16[]{:T(256)} %constant.35.clone.1), dimensions={} | broadcast | bytes 8388610 | tf_op jit(solution)/shard_map/broadcast_in_dim | solution.py:67
  197.6 17.8 %scatter_fusion = bf16[128,256,128]{2,1,0:T(8,128)(2,1)} fusion(bf16[128,256,128]{2,1,0:T(8,128)(2,1)} %broadcast_in_dim.12, s32[96]{0:T(128)S(1)} %fusion.22, bf16[96,256,128]{2,1,0:T(8,128)(2,1)} %copy.43), kind=kCustom, calls=%fused_computation.2 | custom fusion | bytes 18874752 | tf_op jit(solution)/shard_map/scatter | solution.py:69
  215.4 13.9 %all-to-all-start.3 = ((bf16[128,1,256,128]{3,2,1,0:T(8,128)(2,1)}), bf16[128,1,256,128]{3,2,1,0:T(8,128)(2,1)}, u32[]{:S(2)}, u32[]{:S(2)}) async-start(bf16[128,1,256,128]{3,2,1,0:T(8,128)(2,1)} %bitcast.67), calls=%async_computation.3 | async-start | bytes 16777216 | tf_op jit(solution)/shard_map/all_to_all | solution.py:12
  229.3 1.9 copy.47
  231.3 2.4 compare_reduce_fusion
  233.6 95.9 %all-to-all-done.3 = bf16[128,1,256,128]{3,2,1,0:T(8,128)(2,1)} async-done(((bf16[128,1,256,128]{3,2,1,0:T(8,128)(2,1)}), bf16[128,1,256,128]{3,2,1,0:T(8,128)(2,1)}, u32[]{:S(2)}, u32[]{:S(2)}) %all-to-all-start.3) | async-done | bytes 8388640 | tf_op jit(solution)/shard_map/all_to_all | solution.py:12
  329.5 7.9 %fusion = f32[16,256,128]{2,0,1:T(8,128)S(1)} fusion(bf16[128,1,256,128]{3,2,1,0:T(8,128)(2,1)} %all-to-all-done.3, s32[128]{0:T(128)S(1)} %reduce, pred[128]{0:T(512)(128)(4,1)S(1)} %compare_reduce_fusion), kind=kOutput, calls=%fused_computation.3 | convolution fusion | flops 134221824 | bytes 10486400 | tf_op jit(solution)/shard_map/ts,scm->tcm/dot_general | solution.py:76
  337.4 5.0 %bitcast_add_fusion = f32[16,256,128]{1,2,0:T(8,128)} fusion(f32[16,256,128]{1,2,0:T(8,128)S(1)} %copy.47, f32[16,256,128]{2,0,1:T(8,128)S(1)} %fusion, f32[256,256]{1,0:T(8,128)S(1)} %copy-done), kind=kOutput, calls=%fused_computation.9 | convolution fusion | flops 1611137024 | bytes 6553600 | tf_op jit(solution)/shard_map/ct,ncm->ntm/dot_general | solution.py:82
  342.4 2.9 copy.48
  (7 shorter events, 0.1 us)
Async XLA Ops:
  0.0 13.4 %copy-start = (f32[256,256]{1,0:T(8,128)S(1)}, f32[256,256]{1,0:T(8,128)}, u32[]{:S(2)}) copy-start(f32[256,256]{1,0:T(8,128)} %param.9) | copy-start | bytes 786436
  1.9 20.9 %all-to-all-start = ((s32[128,1,1]{2,1,0:T(1,128)}), s32[128,1,1]{2,1,0:T(1,128)S(1)}, u32[]{:S(2)}, u32[]{:S(2)}) async-start(s32[128,1,1]{2,1,0:T(1,128)} %copy.38), calls=%async_computation | async-start | bytes 131072 | tf_op jit(solution)/shard_map/all_to_all | solution.py:37
  22.8 15.6 %all-to-all-start.1 = ((s32[128,1,1]{2,1,0:T(1,128)}), s32[128,1,1]{2,1,0:T(1,128)S(1)}, u32[]{:S(2)}, u32[]{:S(2)}) async-start(s32[128,1,1]{2,1,0:T(1,128)} %copy.39), calls=%async_computation.1 | async-start | bytes 131072 | tf_op jit(solution)/shard_map/all_to_all | solution.py:44
  46.7 9.7 %copy-start.2 = (s32[4,24]{1,0:T(4,128)S(1)}, s32[4,24]{1,0:T(4,128)}, u32[]{:S(2)}) copy-start(s32[4,24]{1,0:T(4,128)} %param.13) | copy-start | bytes 1156
  46.7 9.8 %copy-start.1 = (f32[1024,128]{1,0:T(8,128)S(1)}, f32[1024,128]{1,0:T(8,128)}, u32[]{:S(2)}) copy-start(f32[1024,128]{1,0:T(8,128)} %param.11) | copy-start | bytes 1572868
  46.7 10.0 %copy-start.3 = (f32[1024]{0:T(1024)S(1)}, f32[1024]{0:T(1024)}, u32[]{:S(2)}) copy-start(f32[1024]{0:T(1024)} %param.12) | copy-start | bytes 12292
  46.7 109.8 %all-to-all-start.2 = ((bf16[128,1,256,128]{2,3,1,0:T(8,128)(2,1)}), bf16[128,1,256,128]{2,3,1,0:T(8,128)(2,1)}, u32[]{:S(2)}, u32[]{:S(2)}) async-start(bf16[128,1,256,128]{2,3,1,0:T(8,128)(2,1)} %fusion.2), calls=%async_computation.2 | async-start | bytes 16777216 | tf_op jit(solution)/shard_map/all_to_all | solution.py:8
  215.4 114.1 %all-to-all-start.3 = ((bf16[128,1,256,128]{3,2,1,0:T(8,128)(2,1)}), bf16[128,1,256,128]{3,2,1,0:T(8,128)(2,1)}, u32[]{:S(2)}, u32[]{:S(2)}) async-start(bf16[128,1,256,128]{3,2,1,0:T(8,128)(2,1)} %bitcast.67), calls=%async_computation.3 | async-start | bytes 16777216 | tf_op jit(solution)/shard_map/all_to_all | solution.py:12
where the time goes:
time: 351 us; the launch traced here: 345 us
  waiting for transfers between devices  200 us (57%)
  local copies, waits for them, and re-layouts  55.1 us (16%)
  starting transfers between devices  41.2 us (12%)
  matrix products  35.7 us (10%)
  other arithmetic  13.3 us (4%)
    all_to_all x1, waiting for transfers between devices, route_tiles(): lax.all_to_all(payload, ('obs', 'emis'), split_axis=0, concat_axis=0, til...  99.8 us
    all_to_all x1, waiting for transfers between devices, route_partials(): lax.all_to_all(payload, ('obs', 'emis'), split_axis=0, concat_axis=0, til...  95.9 us
    scatter x1, local copies, waits for them, and re-layouts, per_device(): outgoing = jnp.zeros((slot_count, cells, members), jnp.bfloat16).at[slot_...  17.8 us
    dot_general x1, matrix products, per_device(): jnp.einsum('bkot,bom->bktm', footprints, mismatch, preferred_element_type...  17.7 us
    all_to_all x1, starting transfers between devices, route_partials(): lax.all_to_all(payload, ('obs', 'emis'), split_axis=0, concat_axis=0, til...  13.9 us
    all_to_all x1, starting transfers between devices, per_device(): lax.all_to_all(wanted.reshape(owners, capacity), ('obs', 'emis'), split_a...  11.5 us
    all_to_all x1, starting transfers between devices, route_tiles(): lax.all_to_all(payload, ('obs', 'emis'), split_axis=0, concat_axis=0, til...  9.64 us
    gather x1, local copies, waits for them, and re-layouts, per_device(): arrived.reshape(slot_count, cells, members)[slot_index]  9.45 us
  transfers between devices with their start and end apart: 4, of which 4 were waited for; matrix products, arithmetic and copies ran while one was open for 6% of the time, Pallas kernels for 0%

commit v1 on v0

v1 whole, which is shorter than its diff:
```python
import functools

import jax
import jax.numpy as jnp
from jax import lax
from jax.experimental import pallas as pl
from jax.experimental.pallas import tpu as pltpu
from jax.sharding import PartitionSpec as P

MESH = pl.DeviceIdType.MESH
BF = jnp.bfloat16
F32 = jnp.float32
I32 = jnp.int32
VMEM_BYTES = 60 * 2**20

ORDERS = ((0, 1, 2), (1, 2, 0), (2, 0, 1))


def part_rows(cells):
    third = cells // 48 * 16
    return (cells - 2 * third, third, third)


def steps_of(n):
    return [k for k in (1, 3, 2) if k < n]


def here(n):
    o, e = lax.axis_index("obs"), lax.axis_index("emis")
    return (lax.div(e, 2), lax.div(o, n), lax.rem(o, n)), lax.rem(e, 2)


def device_of(n, xyz, core):
    return (xyz[1] * n + xyz[2], xyz[0] * 2 + core)


def owner_of(n, xyz, core):
    return ((xyz[1] * n + xyz[2]) * n + xyz[0]) * 2 + core


def moved(n, xyz, axis, k):
    return tuple(lax.rem(v + k, n) if a == axis else v for a, v in enumerate(xyz))


def placed(xyz, axis, value):
    return tuple(value if a == axis else v for a, v in enumerate(xyz))


def remote(src, dst, send, recv, device):
    copy = pltpu.make_async_remote_copy(
        src_ref=src, dst_ref=dst, send_sem=send, recv_sem=recv, device_id=device, device_id_type=MESH
    )
    copy.start()
    return copy


def enter(n, xyz, core):
    barrier = pltpu.get_barrier_semaphore()
    count = 0
    for axis in range(3):
        for k in range(1, n):
            for dc in range(2):
                target = device_of(n, moved(n, xyz, axis, k), lax.rem(core + dc, 2))
                pl.semaphore_signal(barrier, inc=1, device_id=target, device_id_type=MESH)
                count += 1
    pl.semaphore_signal(barrier, inc=1, device_id=device_of(n, xyz, 1 - core), device_id_type=MESH)
    pl.semaphore_wait(barrier, count + 1)


def split(value):
    high = value.astype(BF)
    return high, (value - high.astype(F32)).astype(BF)


def dot(a, b):
    return jnp.dot(a, b, preferred_element_type=F32)


def column(row):
    return jnp.broadcast_to(row, (row.shape[1], row.shape[1])).T


def forward_kernel(
    n, rows, ids_ref, control_ref, prior_ref, corr_ref, foot_hbm, obs_ref, weight_ref,
    mm_ref, pair_ref, prev_ref, last_ref,
    g00, g01, g02, g03, g10, g11, g12, g13, g20, g21, g22, g23,
    s0, s1, s2, b0, b1, b2, a0, a1, a2,
    foot, mine, row_ids, table, table_t, table_s,
    foot_sem, id_send, id_recv, table_sem, one_send, one_recv, two_send, two_recv, last_send, last_recv, keep_sem,
):
    gathered = ((g00, g01, g02, g03), (g10, g11, g12, g13), (g20, g21, g22, g23))
    picked, middle, arrived = (s0, s1, s2), (b0, b1, b2), (a0, a1, a2)
    tiles, cells, members = control_ref.shape
    blocks, touched = ids_ref.shape
    xyz, core = here(n)
    steps = steps_of(n)
    starts = (0, rows[0], rows[0] + rows[1])
    lanes = 2 * n * n * n

    load_foot = pltpu.make_async_copy(foot_hbm, foot, foot_sem)
    load_foot.start()

    lane = lax.broadcasted_iota(I32, (8, lanes), 1)
    wanted = jnp.full((8, lanes), tiles, I32)
    pair = jnp.zeros((8, lanes), I32)
    for b in range(blocks):
        for k in range(touched):
            tile = ids_ref[b, k]
            match = lane == lax.div(tile, tiles)
            wanted = jnp.where(match, lax.rem(tile, tiles), wanted)
            pair = jnp.where(match, b * touched + k, pair)
    pair_ref[...] = pair
    mine[...] = wanted
    me = xyz[0] * 2 + core
    row_ids[pl.ds(me, 1)] = wanted[None]

    enter(n, xyz, core)

    sent = []
    row_copies = []
    for dx in range(n):
        for dc in range(2):
            if dx or dc:
                target = device_of(n, moved(n, xyz, 0, dx), lax.rem(core + dc, 2))
                i = dx * 2 + dc
                row_copies.append(remote(mine, row_ids.at[me], id_send.at[i], id_recv.at[i], target))
    sent += row_copies

    corr_h, corr_l = split(corr_ref[...])
    one = {}
    halves = 2
    half = tiles // halves
    for h in range(halves):

        def emit(i, carry, h=h):
            t = h * half + 2 * i
            both = jnp.concatenate([control_ref[t], control_ref[t + 1]], axis=1)
            both_h, both_l = split(both)
            flux = dot(corr_h, both_h) + (dot(corr_h, both_l) + dot(corr_l, both_h))
            for u in range(2):
                prior = prior_ref[pl.ds(t + u, 1), :]
                base = jnp.concatenate(
                    [column(prior[:, members * v : members * (v + 1)]) for v in range(cells // members)], axis=0
                )
                tile = (base + flux[:, members * u : members * (u + 1)]).astype(BF)
                for p in range(3):
                    gathered[p][0][t + u] = tile[starts[p] : starts[p] + rows[p]]
            return carry

        lax.fori_loop(0, half // 2, emit, 0)
        for k in steps:
            for p, order in enumerate(ORDERS):
                i = (p * n + k) * halves + h
                span = pl.ds(h * half, half)
                one[p, k, h] = remote(
                    gathered[p][0].at[span], gathered[p][n - k].at[span], one_send.at[i], one_recv.at[i],
                    device_of(n, moved(n, xyz, order[0], k), core),
                )
                sent.append(one[p, k, h])

    for copy in row_copies:
        copy.wait_recv()
    for e in range(2 * n):
        table[xyz[2], xyz[1], e : e + 1, :] = row_ids[e, 0:1, :]
    at = 2 * n
    copies = []
    for k in steps:
        copies.append(
            remote(table.at[xyz[2], xyz[1]], table.at[xyz[2], xyz[1]], id_send.at[at + k], id_recv.at[at + k],
                   device_of(n, moved(n, xyz, 1, k), core))
        )
    for copy in copies:
        copy.wait_recv()
    sent += copies
    at += n
    copies = []
    for k in steps:
        copies.append(
            remote(table.at[xyz[2]], table.at[xyz[2]], id_send.at[at + k], id_recv.at[at + k],
                   device_of(n, moved(n, xyz, 2, k), core))
        )
    for copy in copies:
        copy.wait_recv()
    sent += copies
    to_scalar = pltpu.make_async_copy(table, table_s, table_sem)
    to_scalar.start()
    to_scalar.wait()

    two = {}
    for j in [0] + steps:
        for p, (first, second, third) in enumerate(ORDERS):
            if j:
                for h in range(halves):
                    one[p, n - j, h].wait_recv()
            source = lax.rem(xyz[first] + j, n)
            owner = owner_of(n, placed(xyz, first, source), core)
            slot = xyz[second] * n + source
            for kk, k in enumerate(steps + [0]):
                column_at = moved(n, xyz, second, k)

                def pick(d, carry, p=p, j=j, k=k, kk=kk, third=third, column_at=column_at, owner=owner, slot=slot):
                    x, y, z = placed(column_at, third, lax.div(d, 2))
                    tile = table_s[z, y, x * 2 + lax.rem(d, 2), owner]
                    value = gathered[p][j][jnp.minimum(tile, tiles - 1)]
                    if k:
                        picked[p][kk, j, d] = value
                    else:
                        middle[p][d, slot] = value
                    return carry

                lax.fori_loop(0, 2 * n, pick, 0)
                if k:
                    i = (p * n + k) * n + j
                    two[p, k, j] = remote(
                        picked[p].at[kk, j], middle[p].at[:, slot], two_send.at[i], two_recv.at[i],
                        device_of(n, column_at, core),
                    )
                    sent.append(two[p, k, j])

    final = []
    kept = []
    for k in [0] + steps:
        if k:
            for p in range(3):
                for j in range(n):
                    two[p, k, j].wait_recv()
        for ds in steps + [0]:
            for dc in range(2):
                for p, (first, second, third) in enumerate(ORDERS):
                    source = lax.rem(xyz[second] + n - k, n)
                    span = pl.ds(source * n, n)
                    mine_at = xyz[third] * 2 + core
                    if ds or dc:
                        goal = moved(n, xyz, third, ds)
                        goal_core = lax.rem(core + dc, 2)
                        i = ((p * n + k) * n + ds) * 2 + dc
                        copy = remote(
                            middle[p].at[goal[third] * 2 + goal_core, span], arrived[p].at[mine_at, span],
                            last_send.at[i], last_recv.at[i], device_of(n, goal, goal_core),
                        )
                        final.append(copy)
                    else:
                        copy = pltpu.make_async_copy(
                            middle[p].at[mine_at, span], arrived[p].at[mine_at, span], keep_sem.at[p * n + k]
                        )
                        copy.start()
                        kept.append(copy)
    sent += final

    flat = table[...].reshape(lanes, lanes)
    table_t[...] = flat.T
    shape = (lanes, lanes)
    coords = []
    for dim in range(2):
        r = lax.broadcasted_iota(I32, shape, dim)
        coords.append(
            ((lax.div(lax.rem(r, 2 * n), 2), lax.rem(lax.div(r, 2 * n), n), lax.div(r, 2 * n * n)), lax.rem(r, 2))
        )
    none = 2 * n * n
    tile_at = lax.broadcasted_iota(I32, (tiles, lanes), 0).astype(F32)
    last_lane = lax.broadcasted_iota(I32, (tiles, lanes), 1)
    lasts = jnp.full((tiles, lanes), float(none), F32)
    prev_ref[...] = jnp.zeros(prev_ref.shape, I32)
    for p, (first, second, third) in enumerate(ORDERS):
        rank = [((c[second] * n + c[third]) * 2 + o).astype(F32) for c, o in coords]
        in_plane = [c[first] == xyz[first] for c, o in coords]
        earlier = (rank[0] < rank[1]) & in_plane[0]
        for j in range(n):
            owner = owner_of(n, moved(n, xyz, first, j), core)
            across = jnp.broadcast_to(table_t[pl.ds(owner, 1), :].astype(F32), shape)
            down = across.T
            before = jnp.max(jnp.where(earlier & (across == down), rank[0], -1.0), axis=0, keepdims=True)
            before = jnp.where(before < 0, float(none), before)
            prev_ref[p * n + j : p * n + j + 1, :] = before.astype(I32)
            hit = (across[:tiles] == tile_at) & in_plane[1][:tiles]
            newest = jnp.max(jnp.where(hit, rank[1][:tiles], -1.0), axis=1, keepdims=True)
            newest = jnp.where(newest < 0, float(none), newest)
            lasts = jnp.where(last_lane == p * n + j, newest, lasts)
    last_ref[...] = lasts.astype(I32)

    load_foot.wait()
    for copy in kept:
        copy.wait()
    for copy in final:
        copy.wait_recv()

    per_block = foot.shape[1]
    for b in range(blocks):

        def add(k, total, b=b):
            tile = lax.div(ids_ref[b, k], tiles)
            oc = lax.rem(tile, 2)
            x = lax.rem(lax.div(tile, 2), n)
            z = lax.rem(lax.div(tile, 2 * n), n)
            y = lax.div(tile, 2 * n * n)
            c = (x, y, z)
            flux = jnp.concatenate(
                [
                    arrived[p][c[third] * 2 + oc, c[second] * n + c[first]]
                    for p, (first, second, third) in enumerate(ORDERS)
                ],
                axis=0,
            )
            return total + dot(foot[b * touched + k], flux)

        modeled = lax.fori_loop(0, touched, add, jnp.zeros((per_block, members), F32), unroll=4)
        per = per_block // members
        weight = jnp.concatenate([column(weight_ref[b * per + v : b * per + v + 1, :]) for v in range(per)], axis=0)
        mm_ref[b] = ((modeled - obs_ref[b * per_block : (b + 1) * per_block, :]) * weight).astype(BF)

    for copy in sent:
        copy.wait_send()


def backward_kernel(
    n, rows, touched, pair_ref, prev_ref, last_ref, mm_ref, control_ref, corr_ref, foot_hbm,
    out_ref,
    p0, p1, p2, b0, b1, b2, c0, c1, c2, h0, h1, h2, q0, q1, q2, r0, r1, r2, o0, o1, o2,
    foot,
    foot_sem, last_send, last_recv, keep_sem, two_send, two_recv, hold_sem, one_send, one_recv,
):
    partial, middle, back, chain = (p0, p1, p2), (b0, b1, b2), (c0, c1, c2), (h0, h1, h2)
    outgoing, incoming, own = (q0, q1, q2), (r0, r1, r2), (o0, o1, o2)
    tiles, cells, members = control_ref.shape
    xyz, core = here(n)
    x, y, z = xyz
    steps = steps_of(n)
    starts = (0, rows[0], rows[0] + rows[1])
    none = 2 * n * n

    load_foot = pltpu.make_async_copy(foot_hbm, foot, foot_sem)
    load_foot.start()
    for p in range(3):
        chain[p][none] = jnp.zeros((rows[p], members), F32)
    enter(n, xyz, core)
    load_foot.wait()

    sent = []
    one_way = {}
    for kz in steps + [0]:
        zo = lax.rem(z + kz, n)

        def make(i, carry, zo=zo):
            oc, xo, yo = lax.rem(i, 2), lax.rem(lax.div(i, 2), n), lax.div(i, 2 * n)
            pair = pair_ref[0, owner_of(n, (xo, yo, zo), oc)]
            value = lax.dot_general(
                foot[pair], mm_ref[lax.div(pair, touched)], (((0,), (0,)), ((), ())), preferred_element_type=F32
            ).astype(BF)
            c = (xo, yo, zo)
            for p, (first, second, third) in enumerate(ORDERS):
                partial[p][c[third] * 2 + oc, c[second], c[first]] = value[starts[p] : starts[p] + rows[p]]
            return carry

        lax.fori_loop(0, 2 * n * n, make, 0, unroll=2)
        for ds in steps + [0]:
            for dc in range(2):
                for p, (first, second, third) in enumerate(ORDERS):
                    if third == 2:
                        if ds != steps[0]:
                            continue
                        ds_here = kz
                        view = lambda ref, block: ref.at[block]
                    elif second == 2:
                        ds_here = ds
                        view = lambda ref, block: ref.at[block, zo]
                    else:
                        ds_here = ds
                        view = lambda ref, block: ref.at[block, :, zo]
                    mine_at = xyz[third] * 2 + core
                    i = ((p * n + kz) * n + ds_here) * 2 + dc
                    if ds_here or dc:
                        goal = moved(n, xyz, third, ds_here)
                        goal_core = lax.rem(core + dc, 2)
                        copy = remote(
                            view(partial[p], goal[third] * 2 + goal_core), view(middle[p], mine_at),
                            last_send.at[i], last_recv.at[i], device_of(n, goal, goal_core),
                        )
                        sent.append(copy)
                    else:
                        copy = pltpu.make_async_copy(
                            view(partial[p], mine_at), view(middle[p], mine_at), keep_sem.at[p * n + kz]
                        )
                        copy.start()
                    one_way.setdefault((p, kz), []).append((copy, bool(ds_here or dc)))

    def arrive(p, kz):
        for copy, far in one_way[p, kz]:
            if far:
                copy.wait_recv()
            else:
                copy.wait()

    two = {}

    def pass_on(p, k, j):
        first, second, third = ORDERS[p]
        goal = moved(n, xyz, second, k)
        to = goal[second]
        row = lax.rem(xyz[first] + j, n)
        src, dst = middle[p].at[:, to, row], back[p].at[row, xyz[second]]
        i = (p * n + k) * n + j
        if k:
            two[p, k, j] = remote(src, dst, two_send.at[i], two_recv.at[i], device_of(n, goal, core))
            sent.append(two[p, k, j])
        else:
            two[p, k, j] = pltpu.make_async_copy(src, dst, hold_sem.at[p * n + j])
            two[p, k, j].start()

    for kz in steps + [0]:
        for p, (first, second, third) in enumerate(ORDERS):
            if second == 2:
                arrive(p, kz)
                for j in steps + [0]:
                    pass_on(p, kz, j)
            elif first == 2:
                arrive(p, kz)
                for k in steps + [0]:
                    pass_on(p, k, kz)
    for p, (first, second, third) in enumerate(ORDERS):
        if third == 2:
            for kz in steps + [0]:
                arrive(p, kz)
            for j in steps + [0]:
                for k in steps + [0]:
                    pass_on(p, k, j)

    one = {}
    for jj, j in enumerate(steps + [0]):
        for p in (1, 2, 0):
            first, second, third = ORDERS[p]
            for k in steps:
                two[p, k, j].wait_recv()
            two[p, 0, j].wait()
            row = lax.rem(xyz[first] + j, n)

            def link(s, carry, p=p, j=j, row=row, first=first, second=second, third=third):
                so, d = lax.div(s, 2 * n), lax.rem(s, 2 * n)
                c = placed(placed(xyz, second, so), third, lax.div(d, 2))
                device = (c[2] * n + c[1]) * (2 * n) + c[0] * 2 + lax.rem(d, 2)
                before = prev_ref[p * n + j, device]
                chain[p][s] = back[p][row, so, d].astype(F32) + chain[p][before]
                return carry

            lax.fori_loop(0, none, link, 0)

            def collect(t, carry, p=p, j=j, jj=jj):
                total = chain[p][last_ref[t, p * n + j]]
                if j:
                    outgoing[p][jj, t] = total.astype(BF)
                else:
                    own[p][t] = total
                return carry

            lax.fori_loop(0, tiles, collect, 0)
            if j:
                i = p * n + j
                one[p, j] = remote(
                    outgoing[p].at[jj], incoming[p].at[jj], one_send.at[i], one_recv.at[i],
                    device_of(n, moved(n, xyz, first, j), core),
                )
                sent.append(one[p, j])

    for copy in one.values():
        copy.wait_recv()

    corr_h, corr_l = split(corr_ref[...].T)

    def finish(i, carry):
        t = 2 * i
        sums = []
        for u in range(2):
            sums.append(
                jnp.concatenate(
                    [
                        own[p][t + u] + sum(incoming[p][jj, t + u].astype(F32) for jj in range(n - 1))
                        for p in range(3)
                    ],
                    axis=0,
                )
            )
        both_h, both_l = split(jnp.concatenate(sums, axis=1))
        spread = dot(corr_h, both_h) + (dot(corr_h, both_l) + dot(corr_l, both_h))
        for u in range(2):
            out_ref[t + u] = control_ref[t + u] + spread[:, members * u : members * (u + 1)]
        return carry

    lax.fori_loop(0, tiles // 2, finish, 0)

    for copy in sent:
        copy.wait_send()


def per_device(n, control, prior_flux, correlation, footprints, obs_values, obs_weights, tile_ids):
    tiles, cells, members = control.shape
    blocks, touched = tile_ids.shape
    per_block = footprints.shape[2]
    owners = 2 * n * n * n
    rows = part_rows(cells)
    foot = footprints.reshape(blocks * touched, per_block, cells)
    vmem, smem, anywhere = (
        pl.BlockSpec(memory_space=pltpu.VMEM),
        pl.BlockSpec(memory_space=pltpu.SMEM),
        pl.BlockSpec(memory_space=pl.ANY),
    )
    dma = pltpu.SemaphoreType.DMA
    foot_scratch = pltpu.VMEM((blocks * touched, per_block, cells), BF)
    mm, pair, prev, last = pl.pallas_call(
        functools.partial(forward_kernel, n, rows),
        name="forward",
        out_shape=(
            jax.ShapeDtypeStruct((blocks, per_block, members), BF),
            jax.ShapeDtypeStruct((8, owners), I32),
            jax.ShapeDtypeStruct((16, owners), I32),
            jax.ShapeDtypeStruct((tiles, owners), I32),
        ),
        in_specs=[smem, vmem, vmem, vmem, anywhere, vmem, vmem],
        out_specs=(vmem,) * 4,
        scratch_shapes=(
            [pltpu.VMEM((tiles, r, members), BF) for r in rows for _ in range(4)]
            + [pltpu.VMEM((n - 1, n, 2 * n, r, members), BF) for r in rows]
            + [pltpu.VMEM((2 * n, n * n, r, members), BF) for r in rows]
            + [pltpu.VMEM((2 * n, n * n, r, members), BF) for r in rows]
            + [
                foot_scratch,
                pltpu.VMEM((8, owners), I32),
                pltpu.VMEM((2 * n, 8, owners), I32),
                pltpu.VMEM((n, n, 2 * n, owners), I32),
                pltpu.VMEM((owners, owners), I32),
                pltpu.SMEM((n, n, 2 * n, owners), I32),
                dma(()), dma((4 * n,)), dma((4 * n,)), dma(()),
                dma((6 * n,)), dma((6 * n,)),
                dma((3 * n * n,)), dma((3 * n * n,)),
                dma((6 * n * n,)), dma((6 * n * n,)),
                dma((3 * n,)),
            ]
        ),
        compiler_params=pltpu.CompilerParams(
            collective_id=0, has_side_effects=True, vmem_limit_bytes=VMEM_BYTES
        ),
    )(tile_ids, control, prior_flux, correlation, foot, obs_values, obs_weights.reshape(-1, members))
    return pl.pallas_call(
        functools.partial(backward_kernel, n, rows, touched),
        name="backward",
        out_shape=jax.ShapeDtypeStruct(control.shape, F32),
        in_specs=[smem, smem, smem, vmem, vmem, vmem, anywhere],
        out_specs=vmem,
        scratch_shapes=(
            [pltpu.VMEM((2 * n, n, n, r, members), BF) for r in rows]
            + [pltpu.VMEM((2 * n, n, n, r, members), BF) for r in rows]
            + [pltpu.VMEM((n, n, 2 * n, r, members), BF) for r in rows]
            + [pltpu.VMEM((2 * n * n + 1, r, members), F32) for r in rows]
            + [pltpu.VMEM((n - 1, tiles, r, members), BF) for r in rows]
            + [pltpu.VMEM((n - 1, tiles, r, members), BF) for r in rows]
            + [pltpu.VMEM((tiles, r, members), F32) for r in rows]
            + [
                foot_scratch,
                dma(()),
                dma((6 * n * n,)), dma((6 * n * n,)), dma((3 * n,)),
                dma((3 * n * n,)), dma((3 * n * n,)), dma((3 * n,)),
                dma((3 * n,)), dma((3 * n,)),
            ]
        ),
        compiler_params=pltpu.CompilerParams(
            collective_id=1, has_side_effects=True, vmem_limit_bytes=VMEM_BYTES
        ),
    )(pair, prev, last, mm, control, correlation, foot)


def solution(mesh):
    n = mesh.shape["emis"] // 2
    return jax.shard_map(
        functools.partial(per_device, n),
        mesh=mesh,
        in_specs=(
            P(("obs", "emis"), None, None),
            P(("obs", "emis"), None),
            P(),
            P(("obs", "emis"), None, None, None),
            P(("obs", "emis"), None),
            P(("obs", "emis")),
            P(("obs", "emis"), None),
        ),
        out_specs=P(("obs", "emis"), None, None),
        check_vma=False,
    )
```

time: 351 us -> 220 us (0.63)
  Pallas kernels: 0 us -> 213 us
  waiting for transfers between devices: 200 us -> 0 us
  local copies, waits for them, and re-layouts: 55.1 us -> 3.11 us
  starting transfers between devices: 41.2 us -> 0 us
  matrix products: 35.7 us -> 0 us
  other arithmetic: 13.3 us -> 0 us
    pallas_call x0 -> x2, Pallas kernels: none -> 213 us  [the longest x1 109 us: per_device(): pl.pallas_call(functools.partial(forward_kernel, n, rows), name='forward'...]
    all_to_all x4 -> x0, waiting for transfers between devices: 200 us -> none  [the longest x1 99.8 us: route_tiles(): lax.all_to_all(payload, ('obs', 'emis'), split_axis=0, concat_axis=0, til...]
    all_to_all x4 -> x0, starting transfers between devices: 41.2 us -> none  [the longest x1 13.9 us: route_partials(): lax.all_to_all(payload, ('obs', 'emis'), split_axis=0, concat_axis=0, til...]
    dot_general x4 -> x0, matrix products: 35.7 us -> none  [the longest x1 17.7 us: per_device(): jnp.einsum('bkot,bom->bktm', footprints, mismatch, preferred_element_type...]
    scatter x1 -> x0, local copies, waits for them, and re-layouts: 17.8 us -> none  [per_device(): outgoing = jnp.zeros((slot_count, cells, members), jnp.bfloat16).at[slot_...]
    gather x2 -> x0, local copies, waits for them, and re-layouts: 16 us -> none  [the longest x1 9.45 us: per_device(): arrived.reshape(slot_count, cells, members)[slot_index]]
    reshape x4 -> x0, local copies, waits for them, and re-layouts: 9.65 us -> none  [the longest x1 8.56 us: per_device(): partial_value.reshape(request_count, cells, members)]
    mul x1 -> x0, other arithmetic: 7.25 us -> none  [per_device(): picked = emission_bf[got_tile] * got_use[:, None, None].astype(jnp.bfloat16)]
  transfers between devices with their start and end apart: 4 -> 0, of which waited for: 4 -> 0; matrix products, arithmetic and copies ran while one was open for 6% -> 0% of each run, Pallas kernels for 0% -> 0%
where the time goes in v1:
time: 220 us; the launch traced here: 216 us
  Pallas kernels  213 us (97%)
  local copies, waits for them, and re-layouts  3.11 us (1%)
    pallas_call x1, Pallas kernels, per_device(): pl.pallas_call(functools.partial(forward_kernel, n, rows), name='forward'...  109 us
    pallas_call x1, Pallas kernels, per_device(): pl.pallas_call(functools.partial(backward_kernel, n, rows, touched), name...  104 us

profile of v1, /device:TPU:1, one launch (start us, length us, event | category | flops | bytes accessed | tf_op | source)
XLA Modules:
  0.0 215.9 jit_solution(6905591619210381446)
XLA Ops:
  0.0 109.2 %forward.1 = (bf16[4,256,128]{2,1,0:T(8,128)(2,1)}, s32[8,128]{1,0:T(8,128)}, s32[16,128]{1,0:T(8,128)}, s32[16,128]{1,0:T(8,128)}) custom-call(s32[4,24]{1,0:T(4,128)} %ids_ref.1, f32[16,256,128]{2,1,0:T(8,128)} %control_ref.3, f32[16,256]{1,0:T(8,128)} %prior_ref.1, f32[256,256]{1,0:T(8,128)} %corr_ref.3, bf16[96,256,256]{2,1,0:T(8,128)(2,1)} %bitcast.2, ...), custom_call_target="tpu_custom_call" | custom-call | tf_op jit(solution)/shard_map/forward/pallas_call | solution.py:507
  109.2 103.6 %backward.1 = f32[16,256,128]{2,1,0:T(8,128)} custom-call(s32[8,128]{1,0:T(8,128)} %get-tuple-element.9.pair_ref, s32[16,128]{1,0:T(8,128)} %get-tuple-element.10.prev_ref, s32[16,128]{1,0:T(8,128)} %get-tuple-element.11.last_ref, bf16[4,256,128]{2,1,0:T(8,128)(2,1)} %get-tuple-element.12.mm_ref, f32[16,256,128]{2,1,0:T(8,128)} %control_ref.3, ...), custom_call_target="tpu_custom_call" | custom-call | tf_op jit(solution)/shard_map/backward/pallas_call | solution.py:541
  212.8 3.1 %copy.9 = f32[16,256,128]{2,1,0:T(8,128)} copy(f32[16,256,128]{2,1,0:T(8,128)} %backward.1) | data formatting | bytes 4194304

commit v2 on v1

v2 whole, which is shorter than its diff:
```python
import functools

import jax
import jax.numpy as jnp
from jax import lax
from jax.experimental import pallas as pl
from jax.experimental.pallas import tpu as pltpu
from jax.sharding import PartitionSpec as P

MESH = pl.DeviceIdType.MESH
BF = jnp.bfloat16
F32 = jnp.float32
I32 = jnp.int32
VMEM_BYTES = 60 * 2**20

ORDERS = ((0, 1, 2), (1, 2, 0), (2, 0, 1))


def part_rows(cells):
    third = cells // 48 * 16
    return (cells - 2 * third, third, third)


STEPS = (1, 3, 2)
BACK = (2, 1, 3)


def here(n):
    o, e = lax.axis_index("obs"), lax.axis_index("emis")
    return (lax.div(e, 2), lax.div(o, n), lax.rem(o, n)), lax.rem(e, 2)


def device_of(n, xyz, core):
    return (xyz[1] * n + xyz[2], xyz[0] * 2 + core)


def owner_of(n, xyz, core):
    return ((xyz[1] * n + xyz[2]) * n + xyz[0]) * 2 + core


def moved(n, xyz, axis, k):
    return tuple(lax.rem(v + k, n) if a == axis else v for a, v in enumerate(xyz))


def placed(xyz, axis, value):
    return tuple(value if a == axis else v for a, v in enumerate(xyz))


def remote(src, dst, send, recv, device):
    copy = pltpu.make_async_remote_copy(
        src_ref=src, dst_ref=dst, send_sem=send, recv_sem=recv, device_id=device, device_id_type=MESH
    )
    copy.start()
    return copy


def line_partners(n, xyz, core):
    for axis in range(3):
        for k in range(1, n):
            for dc in range(2):
                yield device_of(n, moved(n, xyz, axis, k), lax.rem(core + dc, 2))
    yield device_of(n, xyz, 1 - core)


def partners(n, xyz, core):
    yield from line_partners(n, xyz, core)
    for dy in range(1, n):
        for dz in range(1, n):
            yield device_of(n, moved(n, moved(n, xyz, 1, dy), 2, dz), core)


def split(value):
    high = value.astype(BF)
    return high, (value - high.astype(F32)).astype(BF)


def dot(a, b):
    return jnp.dot(a, b, preferred_element_type=F32)


def column(row):
    return jnp.broadcast_to(row, (row.shape[1], row.shape[1])).T


def kernel(
    n, rows, ids_ref, prior_ref, corr_ref, weight_ref, control_hbm, foot_hbm, obs_hbm,
    out_hbm,
    g00, g01, g02, g03, g10, g11, g12, g13, g20, g21, g22, g23,
    s0, s1, s2, b0, b1, b2, a0, a1, a2, h0, h1, h2, r0, r1, r2, m0, m1, m2, o0, o1, o2,
    foot, control, obs, out, mismatch, mine, row_ids, table, table_t, pair_v, prev_v, last_v,
    table_s, pair_s, prev_s, last_s,
    load_sem, id_send, id_recv, scalar_sem, one_send, one_recv, two_send, two_recv, three_send, three_recv, keep_sem,
    back_three_send, back_three_recv, back_keep_sem, back_two_send, back_two_recv, back_one_send, back_one_recv,
    out_sem, free_sem,
):
    gathered = ((g00, g01, g02, g03), (g10, g11, g12, g13), (g20, g21, g22, g23))
    picked, middle, arrived = (s0, s1, s2), (b0, b1, b2), (a0, a1, a2)
    chain, sums_in, relay, own = (h0, h1, h2), (r0, r1, r2), (m0, m1, m2), (o0, o1, o2)
    tiles, cells, members = control.shape
    blocks, touched = ids_ref.shape
    per_block = foot.shape[1]
    xyz, core = here(n)
    starts = (0, rows[0], rows[0] + rows[1])
    lanes = 2 * n * n * n
    none = 2 * n * n
    half = tiles // 2
    halves = (pl.ds(0, half), pl.ds(half, half))

    barrier = pltpu.get_barrier_semaphore()
    count = 0
    for target in partners(n, xyz, core):
        pl.semaphore_signal(barrier, inc=1, device_id=target, device_id_type=MESH)
        count += 1

    loads = []
    for i, (src, dst) in enumerate(((control_hbm, control), (foot_hbm, foot), (obs_hbm, obs))):
        loads.append(pltpu.make_async_copy(src, dst, load_sem.at[i]))
        loads[-1].start()
    load_control, load_foot, load_obs = loads

    lane = lax.broadcasted_iota(I32, (8, lanes), 1)
    wanted = jnp.full((8, lanes), tiles, I32)
    pair = jnp.zeros((8, lanes), I32)
    for b in range(blocks):
        for k in range(touched):
            tile = ids_ref[b, k]
            match = lane == lax.div(tile, tiles)
            wanted = jnp.where(match, lax.rem(tile, tiles), wanted)
            pair = jnp.where(match, b * touched + k, pair)
    pair_v[...] = pair
    mine[...] = wanted
    me = xyz[0] * 2 + core
    row_ids[pl.ds(me, 1)] = wanted[None]
    to_scalar = [pltpu.make_async_copy(pair_v, pair_s, scalar_sem.at[0])]
    to_scalar[0].start()

    corr_h, corr_l = split(corr_ref[...])
    load_control.wait()

    def emit(i, carry):
        t = 2 * i
        both = jnp.concatenate([control[t], control[t + 1]], axis=1)
        both_h, both_l = split(both)
        flux = dot(corr_h, both_h) + (dot(corr_h, both_l) + dot(corr_l, both_h))
        for u in range(2):
            prior = prior_ref[pl.ds(t + u, 1), :]
            base = jnp.concatenate(
                [column(prior[:, members * v : members * (v + 1)]) for v in range(cells // members)], axis=0
            )
            tile = (base + flux[:, members * u : members * (u + 1)]).astype(BF)
            for p in range(3):
                gathered[p][0][t + u] = tile[starts[p] : starts[p] + rows[p]]
        return carry

    lax.fori_loop(0, tiles // 2, emit, 0)

    pl.semaphore_wait(barrier, count)

    sent = []
    row_copies = []
    for dx in range(n):
        for dc in range(2):
            if dx or dc:
                target = device_of(n, moved(n, xyz, 0, dx), lax.rem(core + dc, 2))
                i = dx * 2 + dc
                row_copies.append(remote(mine, row_ids.at[me], id_send.at[i], id_recv.at[i], target))
    sent += row_copies

    one = {}

    def gather(p, k, j, h):
        i = (p * n + (j - k) % n) * 2 + h
        one[p, (j - k) % n, h] = remote(
            gathered[p][j].at[halves[h]], gathered[p][(j - k) % n].at[halves[h]], one_send.at[i], one_recv.at[i],
            device_of(n, moved(n, xyz, ORDERS[p][0], k), core),
        )
        sent.append(one[p, (j - k) % n, h])

    for p in range(3):
        gather(p, 3, 0, 0)
        gather(p, 1, 0, 1)

    for copy in row_copies:
        copy.wait_recv()
    for e in range(2 * n):
        table[xyz[2], xyz[1], e : e + 1, :] = row_ids[e, 0:1, :]
    plane_copies = []
    at = 2 * n
    for dy in range(n):
        for dz in range(n):
            if dy or dz:
                target = device_of(n, moved(n, moved(n, xyz, 1, dy), 2, dz), core)
                i = at + dy * n + dz
                here_ids = table.at[xyz[2], xyz[1]]
                plane_copies.append(remote(here_ids, here_ids, id_send.at[i], id_recv.at[i], target))
    sent += plane_copies

    for p in range(3):
        gather(p, 3, 0, 1)
        gather(p, 1, 0, 0)
    for p in range(3):
        one[p, 1, 0].wait_recv()
        gather(p, 3, 1, 0)
        one[p, 3, 1].wait_recv()
        gather(p, 1, 3, 1)

    for copy in plane_copies:
        copy.wait_recv()
    table_copy = pltpu.make_async_copy(table, table_s, scalar_sem.at[1])
    table_copy.start()
    table_copy.wait()

    two = {}
    for j in (0,) + STEPS:
        for p, (first, second, third) in enumerate(ORDERS):
            if j == 2:
                one[p, 2, 0].wait_recv()
                one[p, 2, 1].wait_recv()
            elif j:
                one[p, j, 1 if j == 1 else 0].wait_recv()
            source = lax.rem(xyz[first] + j, n)
            owner = owner_of(n, placed(xyz, first, source), core)
            for kk, k in enumerate(STEPS + (0,)):
                column_at = moved(n, xyz, second, k)

                def pick(d, carry, p=p, j=j, k=k, kk=kk, third=third, column_at=column_at, owner=owner, source=source,
                         second=second):
                    x, y, z = placed(column_at, third, lax.div(d, 2))
                    tile = table_s[z, y, x * 2 + lax.rem(d, 2), owner]
                    value = gathered[p][j][jnp.clip(tile, 0, tiles - 1)]
                    if k:
                        picked[p][kk, j, d] = value
                    else:
                        middle[p][d, xyz[second], source] = value
                    return carry

                lax.fori_loop(0, 2 * n, pick, 0)
                if k:
                    i = (p * n + k) * n + j
                    two[p, k, j] = remote(
                        picked[p].at[kk, j], middle[p].at[:, xyz[second], source], two_send.at[i], two_recv.at[i],
                        device_of(n, column_at, core),
                    )
                    sent.append(two[p, k, j])

    final = []
    kept = []
    for k in (0,) + STEPS:
        if k:
            for p in range(3):
                for j in range(n):
                    two[p, k, j].wait_recv()
        for ds in STEPS + (0,):
            for dc in range(2):
                for p, (first, second, third) in enumerate(ORDERS):
                    source = lax.rem(xyz[second] + n - k, n)
                    mine_at = xyz[third] * 2 + core
                    if ds or dc:
                        goal = moved(n, xyz, third, ds)
                        goal_core = lax.rem(core + dc, 2)
                        i = ((p * n + k) * n + ds) * 2 + dc
                        copy = remote(
                            middle[p].at[goal[third] * 2 + goal_core, source], arrived[p].at[mine_at, source],
                            three_send.at[i], three_recv.at[i], device_of(n, goal, goal_core),
                        )
                        final.append(copy)
                    else:
                        copy = pltpu.make_async_copy(
                            middle[p].at[mine_at, source], arrived[p].at[mine_at, source], keep_sem.at[p * n + k]
                        )
                        copy.start()
                        kept.append(copy)
    sent += final

    table_t[...] = table[...].reshape(lanes, lanes).T
    shape = (lanes, lanes)
    coords = []
    for dim in range(2):
        r = lax.broadcasted_iota(I32, shape, dim)
        coords.append(
            ((lax.div(lax.rem(r, 2 * n), 2), lax.rem(lax.div(r, 2 * n), n), lax.div(r, 2 * n * n)), lax.rem(r, 2))
        )
    tile_at = lax.broadcasted_iota(I32, (tiles, lanes), 0)
    last_lane = lax.broadcasted_iota(I32, (tiles, lanes), 1)
    lasts = jnp.full((tiles, lanes), none, I32)
    prev_v[...] = jnp.zeros(prev_v.shape, I32)
    for p, (first, second, third) in enumerate(ORDERS):
        rank = [
            (lax.rem(c[second] + (n - xyz[second]), n) * n + c[third]) * 2 + o for c, o in coords
        ]
        in_plane = [c[first] == xyz[first] for c, o in coords]
        earlier = (rank[0] < rank[1]) & in_plane[0]
        for j in range(n):
            owner = owner_of(n, moved(n, xyz, first, j), core)
            across = jnp.broadcast_to(table_t[pl.ds(owner, 1), :], shape)
            down = across.T
            before = jnp.max(jnp.where(earlier & (across == down), rank[0], -1), axis=0, keepdims=True)
            prev_v[p * n + j : p * n + j + 1, :] = jnp.where(before < 0, none, before)
            hit = (across[:tiles] == tile_at) & in_plane[1][:tiles]
            newest = jnp.max(jnp.where(hit, rank[1][:tiles], -1), axis=1, keepdims=True)
            newest = jnp.where(newest < 0, none, newest)
            lasts = jnp.where(last_lane == p * n + j, newest, lasts)
    last_v[...] = lasts
    for i, (src, dst) in enumerate(((prev_v, prev_s), (last_v, last_s))):
        to_scalar.append(pltpu.make_async_copy(src, dst, scalar_sem.at[2 + i]))
        to_scalar[-1].start()
    for p in range(3):
        chain[p][none] = jnp.zeros((rows[p], members), F32)

    load_foot.wait()
    load_obs.wait()
    for copy in to_scalar + kept:
        copy.wait()
    for copy in final:
        copy.wait_recv()
    for copy in sent:
        copy.wait_send()
    freed = 0
    for target in line_partners(n, xyz, core):
        pl.semaphore_signal(free_sem, inc=1, device_id=target, device_id_type=MESH)
        freed += 1

    per = per_block // members

    def model(b, carry):
        feet, flux = [], []
        for k in range(touched):
            tile = lax.div(ids_ref[b, k], tiles)
            oc = lax.rem(tile, 2)
            c = (lax.rem(lax.div(tile, 2), n), lax.div(tile, 2 * n * n), lax.rem(lax.div(tile, 2 * n), n))
            for p, (first, second, third) in enumerate(ORDERS):
                flux.append(arrived[p][c[third] * 2 + oc, c[second], c[first]])
            feet.append(foot[b * touched + k])
        modeled = dot(jnp.concatenate(feet, axis=1), jnp.concatenate(flux, axis=0))
        weight = jnp.concatenate([column(weight_ref[pl.ds(b * per + v, 1), :]) for v in range(per)], axis=0)
        wrong = (modeled - obs[pl.ds(pl.multiple_of(b * per_block, per_block), per_block), :]) * weight
        mismatch[b] = wrong.T.astype(BF)
        return carry

    lax.fori_loop(0, blocks, model, 0)

    sent = []
    one_way = {}
    for kz in BACK + (0,):
        zo = lax.rem(xyz[2] + kz, n)

        def make(i, carry, zo=zo):
            oc, xo, yo = lax.rem(i, 2), lax.rem(lax.div(i, 2), n), lax.div(i, 2 * n)
            pair = jnp.clip(pair_s[0, owner_of(n, (xo, yo, zo), oc)], 0, blocks * touched - 1)
            value = dot(mismatch[lax.div(pair, touched)], foot[pair]).astype(BF).T
            c = (xo, yo, zo)
            for p, (first, second, third) in enumerate(ORDERS):
                arrived[p][c[third] * 2 + oc, c[second], c[first]] = value[starts[p] : starts[p] + rows[p]]
            return carry

        lax.fori_loop(0, 2 * n * n, make, 0, unroll=4)
        if kz == BACK[0]:
            pl.semaphore_wait(free_sem, freed)
        for ds in STEPS + (0,):
            for dc in range(2):
                for p, (first, second, third) in enumerate(ORDERS):
                    if third == 2:
                        if ds != STEPS[0]:
                            continue
                        step = kz
                        view = lambda ref, block: ref.at[block]
                    elif second == 2:
                        step = ds
                        view = lambda ref, block: ref.at[block, zo]
                    else:
                        step = ds
                        view = lambda ref, block: ref.at[block, :, zo]
                    mine_at = xyz[third] * 2 + core
                    i = ((p * n + kz) * n + step) * 2 + dc
                    far = bool(step or dc)
                    if far:
                        goal = moved(n, xyz, third, step)
                        goal_core = lax.rem(core + dc, 2)
                        copy = remote(
                            view(arrived[p], goal[third] * 2 + goal_core), view(middle[p], mine_at),
                            back_three_send.at[i], back_three_recv.at[i], device_of(n, goal, goal_core),
                        )
                        sent.append(copy)
                    else:
                        copy = pltpu.make_async_copy(
                            view(arrived[p], mine_at), view(middle[p], mine_at), back_keep_sem.at[p * n + kz]
                        )
                        copy.start()
                    one_way.setdefault((p, kz), []).append((copy, far))

    def arrive(p, kz):
        for copy, far in one_way[p, kz]:
            if far:
                copy.wait_recv()
            else:
                copy.wait()

    two = {}

    def pass_on(p, k, j):
        first, second, third = ORDERS[p]
        if not k:
            return
        goal = moved(n, xyz, second, k)
        row = lax.rem(xyz[first] + j, n)
        i = (p * n + k) * n + j
        two[p, k, j] = remote(
            middle[p].at[:, goal[second], row], picked[p].at[STEPS.index(n - k), j],
            back_two_send.at[i], back_two_recv.at[i], device_of(n, goal, core),
        )
        sent.append(two[p, k, j])

    for kz in BACK + (0,):
        for p, (first, second, third) in enumerate(ORDERS):
            if second == 2:
                arrive(p, kz)
                for j in BACK + (0,):
                    pass_on(p, kz, j)
            elif first == 2:
                arrive(p, kz)
                for k in STEPS:
                    pass_on(p, k, kz)
    for p, (first, second, third) in enumerate(ORDERS):
        if third == 2:
            for kz in BACK + (0,):
                arrive(p, kz)
            for j in BACK + (0,):
                for k in STEPS:
                    pass_on(p, k, j)

    one = {}
    relayed = {}

    def give(p, k, j, h, key, src, dst, i):
        copy = remote(
            src, dst, back_one_send.at[i], back_one_recv.at[i],
            device_of(n, moved(n, xyz, ORDERS[p][0], k), core),
        )
        sent.append(copy)
        return copy

    for j in (2, 0, 1, 3):
        for p in (1, 2, 0):
            first, second, third = ORDERS[p]
            for k in STEPS:
                two[p, k, j].wait_recv()
            row = lax.rem(xyz[first] + j, n)
            for step in (0, 1, 2, 3):

                def link(d, carry, p=p, j=j, row=row, first=first, second=second, third=third, step=step):
                    so = lax.rem(xyz[second] + step, n)
                    c = placed(placed(xyz, second, so), third, lax.div(d, 2))
                    device = (c[2] * n + c[1]) * (2 * n) + c[0] * 2 + lax.rem(d, 2)
                    before = jnp.clip(prev_s[p * n + j, device], 0, none)
                    if step:
                        value = picked[p][STEPS.index(step), j, d]
                    else:
                        value = middle[p][d, so, row]
                    chain[p][step * 2 * n + d] = value.astype(F32) + chain[p][before]
                    return carry

                lax.fori_loop(0, 2 * n, link, 0)

            for h in range(2):
                joins = (j == 1 and h == 0) or (j == 3 and h == 1)
                if joins:
                    relayed[p, h].wait_recv()

                def collect(t, carry, p=p, j=j, h=h, joins=joins):
                    total = chain[p][jnp.clip(last_s[h * half + t, p * n + j], 0, none)]
                    if joins:
                        total = total + relay[p][h, t].astype(F32)
                    if j:
                        gathered[p][j][h * half + t] = total.astype(BF)
                    else:
                        own[p][h * half + t] = total
                    return carry

                lax.fori_loop(0, half, collect, 0)
                if j == 2:
                    k = 1 if h == 0 else 3
                    relayed[p, h] = give(
                        p, k, j, h, "relay", gathered[p][j].at[halves[h]], relay[p].at[h], (p * n + 2) * 2 + h
                    )
                elif j:
                    one[p, j, h] = give(
                        p, j, j, h, "sum", gathered[p][j].at[halves[h]],
                        sums_in[p].at[0 if j == 1 else 1, halves[h]], (p * n + j) * 2 + h,
                    )

    corr_h, corr_l = split(corr_ref[...].T)
    stores = []
    for h in range(2):
        for p in (1, 2, 0):
            for j in (1, 3):
                one[p, j, h].wait_recv()

        def finish(i, carry, h=h):
            t = h * half + 2 * i
            adjoint = []
            for u in range(2):
                adjoint.append(
                    jnp.concatenate(
                        [
                            own[p][t + u] + (sums_in[p][0, t + u].astype(F32) + sums_in[p][1, t + u].astype(F32))
                            for p in range(3)
                        ],
                        axis=0,
                    )
                )
            both_h, both_l = split(jnp.concatenate(adjoint, axis=1))
            spread = dot(corr_h, both_h) + (dot(corr_h, both_l) + dot(corr_l, both_h))
            for u in range(2):
                out[t + u] = control[t + u] + spread[:, members * u : members * (u + 1)]
            return carry

        lax.fori_loop(0, half // 2, finish, 0)
        stores.append(pltpu.make_async_copy(out.at[halves[h]], out_hbm.at[halves[h]], out_sem.at[h]))
        stores[-1].start()

    for copy in sent:
        copy.wait_send()
    for copy in stores:
        copy.wait()


def per_device(n, control, prior_flux, correlation, footprints, obs_values, obs_weights, tile_ids):
    tiles, cells, members = control.shape
    blocks, touched = tile_ids.shape
    per_block = footprints.shape[2]
    owners = 2 * n * n * n
    rows = part_rows(cells)
    foot = footprints.reshape(blocks * touched, per_block, cells)
    vmem, smem, anywhere = (
        pl.BlockSpec(memory_space=pltpu.VMEM),
        pl.BlockSpec(memory_space=pltpu.SMEM),
        pl.BlockSpec(memory_space=pl.ANY),
    )

    def dma(count):
        return pltpu.SemaphoreType.DMA((count,))

    return pl.pallas_call(
        functools.partial(kernel, n, rows),
        name="gradient",
        out_shape=jax.ShapeDtypeStruct(control.shape, F32),
        in_specs=[smem, vmem, vmem, vmem, anywhere, anywhere, anywhere],
        out_specs=anywhere,
        scratch_shapes=(
            [pltpu.VMEM((tiles, r, members), BF) for r in rows for _ in range(4)]
            + [pltpu.VMEM((n - 1, n, 2 * n, r, members), BF) for r in rows]
            + [pltpu.VMEM((2 * n, n, n, r, members), BF) for r in rows]
            + [pltpu.VMEM((2 * n, n, n, r, members), BF) for r in rows]
            + [pltpu.VMEM((2 * n * n + 1, r, members), F32) for r in rows]
            + [pltpu.VMEM((2, tiles, r, members), BF) for r in rows]
            + [pltpu.VMEM((2, tiles // 2, r, members), BF) for r in rows]
            + [pltpu.VMEM((tiles, r, members), F32) for r in rows]
            + [
                pltpu.VMEM((blocks * touched, per_block, cells), BF),
                pltpu.VMEM(control.shape, F32),
                pltpu.VMEM(obs_values.shape, F32),
                pltpu.VMEM(control.shape, F32),
                pltpu.VMEM((blocks, members, per_block), BF),
                pltpu.VMEM((8, owners), I32),
                pltpu.VMEM((2 * n, 8, owners), I32),
                pltpu.VMEM((n, n, 2 * n, owners), I32),
                pltpu.VMEM((owners, owners), I32),
                pltpu.VMEM((8, owners), I32),
                pltpu.VMEM((16, owners), I32),
                pltpu.VMEM((tiles, owners), I32),
                pltpu.SMEM((n, n, 2 * n, owners), I32),
                pltpu.SMEM((8, owners), I32),
                pltpu.SMEM((16, owners), I32),
                pltpu.SMEM((tiles, owners), I32),
                dma(3), dma(2 * n + n * n), dma(2 * n + n * n), dma(4),
                dma(6 * n), dma(6 * n),
                dma(3 * n * n), dma(3 * n * n),
                dma(6 * n * n), dma(6 * n * n), dma(3 * n),
                dma(6 * n * n), dma(6 * n * n), dma(3 * n),
                dma(3 * n * n), dma(3 * n * n),
                dma(6 * n), dma(6 * n),
                dma(2), pltpu.SemaphoreType.REGULAR,
            ]
        ),
        compiler_params=pltpu.CompilerParams(
            collective_id=0, has_side_effects=True, vmem_limit_bytes=VMEM_BYTES
        ),
    )(tile_ids, prior_flux, correlation, obs_weights.reshape(-1, members), control, foot, obs_values)


def solution(mesh):
    n = mesh.shape["emis"] // 2
    return jax.shard_map(
        functools.partial(per_device, n),
        mesh=mesh,
        in_specs=(
            P(("obs", "emis"), None, None),
            P(("obs", "emis"), None),
            P(),
            P(("obs", "emis"), None, None, None),
            P(("obs", "emis"), None),
            P(("obs", "emis")),
            P(("obs", "emis"), None),
        ),
        out_specs=P(("obs", "emis"), None, None),
        check_vma=False,
    )
```

time: 220 us -> 195 us (0.89); the launches traced: 216 us -> 195 us
  Pallas kernels: 213 us -> 192 us
    pallas_call x2 -> x1, Pallas kernels: 213 us -> 192 us  [per_device(): pl.pallas_call(functools.partial(kernel, n, rows), name='gradient', out_s...]
where the time goes in v2:
time: 195 us
  Pallas kernels  192 us (98%)
  local copies, waits for them, and re-layouts  3.11 us (2%)
    pallas_call x1, Pallas kernels, per_device(): pl.pallas_call(functools.partial(kernel, n, rows), name='gradient', out_s...  192 us

profile of v2, /device:TPU:1, one launch (start us, length us, event | category | flops | bytes accessed | tf_op | source)
XLA Modules:
  0.0 194.8 jit_solution(16880287199399586100)
XLA Ops:
  0.0 191.7 %gradient.1 = f32[16,256,128]{2,1,0:T(8,128)} custom-call(s32[4,24]{1,0:T(4,128)} %ids_ref.1, f32[16,256]{1,0:T(8,128)} %prior_ref.1, f32[256,256]{1,0:T(8,128)} %corr_ref.1, f32[8,128]{1,0:T(8,128)} %bitcast.3, f32[16,256,128]{2,1,0:T(8,128)} %control_hbm.1, bf16[96,256,256]{2,1,0:T(8,128)(2,1)} %bitcast.2, f32[1024,128]{1,0:T(8,128)} %obs_hbm.1), custom_call_target="tpu_custom_call" | custom-call | tf_op jit(solution)/shard_map/gradient/pallas_call | solution.py:543
  191.7 3.1 %copy.9 = f32[16,256,128]{2,1,0:T(8,128)} copy(f32[16,256,128]{2,1,0:T(8,128)} %gradient.1) | data formatting | bytes 4194304

commit v3 on v2

--- a/solution.py
+++ b/solution.py
@@ -16,9 +16,25 @@
 ORDERS = ((0, 1, 2), (1, 2, 0), (2, 0, 1))
 
 
+SHARED = 16
+
+
+def part_starts(cells):
+    third = cells // 48 * 16
+    return (0, third, cells - third)
+
+
 def part_rows(cells):
     third = cells // 48 * 16
-    return (cells - 2 * third, third, third)
+    return (third + SHARED, third + SHARED, third)
+
+
+def sent_rows(rows, p, other):
+    if p == 0 and other:
+        return pl.ds(0, rows[0] - SHARED)
+    if p == 1 and not other:
+        return pl.ds(SHARED, rows[1] - SHARED)
+    return pl.ds(0, rows[p])
 
 
 STEPS = (1, 3, 2)
@@ -100,7 +116,7 @@
     blocks, touched = ids_ref.shape
     per_block = foot.shape[1]
     xyz, core = here(n)
-    starts = (0, rows[0], rows[0] + rows[1])
+    starts = part_starts(cells)
     lanes = 2 * n * n * n
     none = 2 * n * n
     half = tiles // 2
@@ -212,21 +228,22 @@
 
     two = {}
     for j in (0,) + STEPS:
-        for p, (first, second, third) in enumerate(ORDERS):
+        for p in range(3):
             if j == 2:
                 one[p, 2, 0].wait_recv()
                 one[p, 2, 1].wait_recv()
             elif j:
                 one[p, j, 1 if j == 1 else 0].wait_recv()
-            source = lax.rem(xyz[first] + j, n)
-            owner = owner_of(n, placed(xyz, first, source), core)
-            for kk, k in enumerate(STEPS + (0,)):
+        for kk, k in enumerate(STEPS + (0,)):
+            for p, (first, second, third) in enumerate(ORDERS):
+                source = lax.rem(xyz[first] + j, n)
+                owner = owner_of(n, placed(xyz, first, source), core)
                 column_at = moved(n, xyz, second, k)
 
                 def pick(d, carry, p=p, j=j, k=k, kk=kk, third=third, column_at=column_at, owner=owner, source=source,
                          second=second):
-                    x, y, z = placed(column_at, third, lax.div(d, 2))
-                    tile = table_s[z, y, x * 2 + lax.rem(d, 2), owner]
+                    x, y, z = placed(column_at, third, lax.rem(d, n))
+                    tile = table_s[z, y, x * 2 + lax.rem(core + lax.div(d, n), 2), owner]
                     value = gathered[p][j][jnp.clip(tile, 0, tiles - 1)]
                     if k:
                         picked[p][kk, j, d] = value
@@ -236,12 +253,14 @@
 
                 lax.fori_loop(0, 2 * n, pick, 0)
                 if k:
-                    i = (p * n + k) * n + j
-                    two[p, k, j] = remote(
-                        picked[p].at[kk, j], middle[p].at[:, xyz[second], source], two_send.at[i], two_recv.at[i],
-                        device_of(n, column_at, core),
-                    )
-                    sent.append(two[p, k, j])
+                    for other in range(2):
+                        i = ((p * n + k) * n + j) * 2 + other
+                        span, at_rows = pl.ds(other * n, n), sent_rows(rows, p, other)
+                        two[p, k, j, other] = remote(
+                            picked[p].at[kk, j, span, at_rows], middle[p].at[span, xyz[second], source, at_rows],
+                            two_send.at[i], two_recv.at[i], device_of(n, column_at, core),
+                        )
+                        sent.append(two[p, k, j, other])
 
     final = []
     kept = []
@@ -249,27 +268,26 @@
         if k:
             for p in range(3):
                 for j in range(n):
-                    two[p, k, j].wait_recv()
+                    for other in range(2):
+                        two[p, k, j, other].wait_recv()
         for ds in STEPS + (0,):
-            for dc in range(2):
+            for other in range(2):
                 for p, (first, second, third) in enumerate(ORDERS):
                     source = lax.rem(xyz[second] + n - k, n)
-                    mine_at = xyz[third] * 2 + core
-                    if ds or dc:
-                        goal = moved(n, xyz, third, ds)
-                        goal_core = lax.rem(core + dc, 2)
-                        i = ((p * n + k) * n + ds) * 2 + dc
-                        copy = remote(
-                            middle[p].at[goal[third] * 2 + goal_core, source], arrived[p].at[mine_at, source],
-                            three_send.at[i], three_recv.at[i], device_of(n, goal, goal_core),
+                    mine_at = other * n + xyz[third]
+                    at_rows = sent_rows(rows, p, other)
+                    goal = moved(n, xyz, third, ds)
+                    src = middle[p].at[other * n + goal[third], source, :, at_rows]
+                    dst = arrived[p].at[mine_at, source, :, at_rows]
+                    if ds or other:
+                        i = ((p * n + k) * n + ds) * 2 + other
+                        final.append(
+                            remote(src, dst, three_send.at[i], three_recv.at[i],
+                                   device_of(n, goal, lax.rem(core + other, 2)))
                         )
-                        final.append(copy)
                     else:
-                        copy = pltpu.make_async_copy(
-                            middle[p].at[mine_at, source], arrived[p].at[mine_at, source], keep_sem.at[p * n + k]
-                        )
-                        copy.start()
-                        kept.append(copy)
+                        kept.append(pltpu.make_async_copy(src, dst, keep_sem.at[p * n + k]))
+                        kept[-1].start()
     sent += final
 
     table_t[...] = table[...].reshape(lanes, lanes).T
@@ -286,7 +304,8 @@
     prev_v[...] = jnp.zeros(prev_v.shape, I32)
     for p, (first, second, third) in enumerate(ORDERS):
         rank = [
-            (lax.rem(c[second] + (n - xyz[second]), n) * n + c[third]) * 2 + o for c, o in coords
+            (lax.rem(c[second] + (n - xyz[second]), n) * n + c[third]) * 2 + lax.rem(o + core, 2)
+            for c, o in coords
         ]
         in_plane = [c[first] == xyz[first] for c, o in coords]
         earlier = (rank[0] < rank[1]) & in_plane[0]
@@ -328,8 +347,13 @@
             tile = lax.div(ids_ref[b, k], tiles)
             oc = lax.rem(tile, 2)
             c = (lax.rem(lax.div(tile, 2), n), lax.div(tile, 2 * n * n), lax.rem(lax.div(tile, 2 * n), n))
-            for p, (first, second, third) in enumerate(ORDERS):
-                flux.append(arrived[p][c[third] * 2 + oc, c[second], c[first]])
+            other = lax.rem(oc + core, 2)
+            v0, v1, v2 = (
+                arrived[p][other * n + c[third], c[second], c[first]]
+                for p, (first, second, third) in enumerate(ORDERS)
+            )
+            shared = jnp.where(other == 0, v0[rows[0] - SHARED :], v1[:SHARED])
+            flux += [v0[: rows[0] - SHARED], shared, v1[SHARED:], v2]
             feet.append(foot[b * touched + k])
         modeled = dot(jnp.concatenate(feet, axis=1), jnp.concatenate(flux, axis=0))
         weight = jnp.concatenate([column(weight_ref[pl.ds(b * per + v, 1), :]) for v in range(per)], axis=0)
@@ -341,92 +365,63 @@
 
     sent = []
     one_way = {}
-    for kz in BACK + (0,):
-        zo = lax.rem(xyz[2] + kz, n)
-
-        def make(i, carry, zo=zo):
-            oc, xo, yo = lax.rem(i, 2), lax.rem(lax.div(i, 2), n), lax.div(i, 2 * n)
-            pair = jnp.clip(pair_s[0, owner_of(n, (xo, yo, zo), oc)], 0, blocks * touched - 1)
-            value = dot(mismatch[lax.div(pair, touched)], foot[pair]).astype(BF).T
-            c = (xo, yo, zo)
-            for p, (first, second, third) in enumerate(ORDERS):
-                arrived[p][c[third] * 2 + oc, c[second], c[first]] = value[starts[p] : starts[p] + rows[p]]
-            return carry
-
-        lax.fori_loop(0, 2 * n * n, make, 0, unroll=4)
-        if kz == BACK[0]:
-            pl.semaphore_wait(free_sem, freed)
-        for ds in STEPS + (0,):
-            for dc in range(2):
+    for turn in range(n):
+
+        for other in range(2):
+
+            def make(i, carry, turn=turn, other=other):
+                dx, dy = lax.rem(i, n), lax.div(i, n)
+                far = (dx, dy, lax.rem(turn + 2 * n - dx - dy, n))
+                c = tuple(lax.rem(xyz[a] + far[a], n) for a in range(3))
+                pair = jnp.clip(pair_s[0, owner_of(n, c, lax.rem(core + other, 2))], 0, blocks * touched - 1)
+                value = dot(mismatch[lax.div(pair, touched)], foot[pair]).astype(BF).T
                 for p, (first, second, third) in enumerate(ORDERS):
-                    if third == 2:
-                        if ds != STEPS[0]:
-                            continue
-                        step = kz
-                        view = lambda ref, block: ref.at[block]
-                    elif second == 2:
-                        step = ds
-                        view = lambda ref, block: ref.at[block, zo]
-                    else:
-                        step = ds
-                        view = lambda ref, block: ref.at[block, :, zo]
-                    mine_at = xyz[third] * 2 + core
-                    i = ((p * n + kz) * n + step) * 2 + dc
-                    far = bool(step or dc)
-                    if far:
-                        goal = moved(n, xyz, third, step)
-                        goal_core = lax.rem(core + dc, 2)
-                        copy = remote(
-                            view(arrived[p], goal[third] * 2 + goal_core), view(middle[p], mine_at),
-                            back_three_send.at[i], back_three_recv.at[i], device_of(n, goal, goal_core),
-                        )
+                    arrived[p][other * n + c[third], lax.rem(far[second] + far[first], n), c[second]] = (
+                        value[starts[p] : starts[p] + rows[p]]
+                    )
+                return carry
+
+            lax.fori_loop(0, n * n, make, 0, unroll=4)
+            if turn == 0 and other == 0:
+                pl.semaphore_wait(free_sem, freed)
+            for ds in STEPS + (0,):
+                for p, (first, second, third) in enumerate(ORDERS):
+                    goal = moved(n, xyz, third, ds)
+                    at_rows = sent_rows(rows, p, other)
+                    lies = (turn - ds) % n
+                    src = arrived[p].at[other * n + goal[third], lies, :, at_rows]
+                    dst = middle[p].at[other * n + xyz[third], lies, :, at_rows]
+                    if ds or other:
+                        i = ((p * n + turn) * n + ds) * 2 + other
+                        copy = remote(src, dst, back_three_send.at[i], back_three_recv.at[i],
+                                      device_of(n, goal, lax.rem(core + other, 2)))
                         sent.append(copy)
                     else:
-                        copy = pltpu.make_async_copy(
-                            view(arrived[p], mine_at), view(middle[p], mine_at), back_keep_sem.at[p * n + kz]
-                        )
+                        copy = pltpu.make_async_copy(src, dst, back_keep_sem.at[p * n + turn])
                         copy.start()
-                    one_way.setdefault((p, kz), []).append((copy, far))
-
-    def arrive(p, kz):
-        for copy, far in one_way[p, kz]:
+                    one_way.setdefault(p, []).append((copy, bool(ds or other)))
+
+    for p in range(3):
+        for copy, far in one_way[p]:
             if far:
                 copy.wait_recv()
             else:
                 copy.wait()
 
     two = {}
-
-    def pass_on(p, k, j):
-        first, second, third = ORDERS[p]
-        if not k:
-            return
-        goal = moved(n, xyz, second, k)
-        row = lax.rem(xyz[first] + j, n)
-        i = (p * n + k) * n + j
-        two[p, k, j] = remote(
-            middle[p].at[:, goal[second], row], picked[p].at[STEPS.index(n - k), j],
-            back_two_send.at[i], back_two_recv.at[i], device_of(n, goal, core),
-        )
-        sent.append(two[p, k, j])
-
-    for kz in BACK + (0,):
-        for p, (first, second, third) in enumerate(ORDERS):
-            if second == 2:
-                arrive(p, kz)
-                for j in BACK + (0,):
-                    pass_on(p, kz, j)
-            elif first == 2:
-                arrive(p, kz)
-                for k in STEPS:
-                    pass_on(p, k, kz)
-    for p, (first, second, third) in enumerate(ORDERS):
-        if third == 2:
-            for kz in BACK + (0,):
-                arrive(p, kz)
-            for j in BACK + (0,):
-                for k in STEPS:
-                    pass_on(p, k, j)
+    for j in BACK + (0,):
+        for k in STEPS:
+            for p, (first, second, third) in enumerate(ORDERS):
+                goal = moved(n, xyz, second, k)
+                for other in range(2):
+                    span, at_rows = pl.ds(other * n, n), sent_rows(rows, p, other)
+                    i = ((p * n + k) * n + j) * 2 + other
+                    two[p, k, j, other] = remote(
+                        middle[p].at[span, (k + j) % n, goal[second], at_rows],
+                        picked[p].at[STEPS.index(n - k), j, span, at_rows],
+                        back_two_send.at[i], back_two_recv.at[i], device_of(n, goal, core),
+                    )
+                    sent.append(two[p, k, j, other])
 
     one = {}
     relayed = {}
@@ -439,27 +434,33 @@
         sent.append(copy)
         return copy
 
-    for j in (2, 0, 1, 3):
+    for j in BACK + (0,):
         for p in (1, 2, 0):
             first, second, third = ORDERS[p]
             for k in STEPS:
-                two[p, k, j].wait_recv()
-            row = lax.rem(xyz[first] + j, n)
-            for step in (0, 1, 2, 3):
-
-                def link(d, carry, p=p, j=j, row=row, first=first, second=second, third=third, step=step):
+                for other in range(2):
+                    two[p, k, j, other].wait_recv()
+            for step in range(n):
+
+                def link(third_at, carry, p=p, j=j, first=first, second=second, third=third, step=step):
                     so = lax.rem(xyz[second] + step, n)
-                    c = placed(placed(xyz, second, so), third, lax.div(d, 2))
-                    device = (c[2] * n + c[1]) * (2 * n) + c[0] * 2 + lax.rem(d, 2)
-                    before = jnp.clip(prev_s[p * n + j, device], 0, none)
-                    if step:
-                        value = picked[p][STEPS.index(step), j, d]
-                    else:
-                        value = middle[p][d, so, row]
-                    chain[p][step * 2 * n + d] = value.astype(F32) + chain[p][before]
+                    c = placed(placed(xyz, second, so), third, third_at)
+                    for other in range(2):
+                        d = other * n + third_at
+                        device = (c[2] * n + c[1]) * (2 * n) + c[0] * 2 + lax.rem(core + other, 2)
+                        before = jnp.clip(prev_s[p * n + j, device], 0, none)
+                        at = sent_rows(rows, p, other)
+                        if step:
+                            value = picked[p][STEPS.index(step), j, d, at]
+                        else:
+                            value = middle[p][d, j, so, at]
+                        chain[p][(step * n + third_at) * 2 + other, at] = value.astype(F32) + chain[p][before, at]
+                        if at.size < rows[p]:
+                            rest = pl.ds(at.size if at.start == 0 else 0, rows[p] - at.size)
+                            chain[p][(step * n + third_at) * 2 + other, rest] = chain[p][before, rest]
                     return carry
 
-                lax.fori_loop(0, 2 * n, link, 0)
+                lax.fori_loop(0, n, link, 0)
 
             for h in range(2):
                 joins = (j == 1 and h == 0) or (j == 3 and h == 1)
@@ -499,15 +500,12 @@
             t = h * half + 2 * i
             adjoint = []
             for u in range(2):
-                adjoint.append(
-                    jnp.concatenate(
-                        [
-                            own[p][t + u] + (sums_in[p][0, t + u].astype(F32) + sums_in[p][1, t + u].astype(F32))
-                            for p in range(3)
-                        ],
-                        axis=0,
-                    )
+                v0, v1, v2 = (
+                    own[p][t + u] + (sums_in[p][0, t + u].astype(F32) + sums_in[p][1, t + u].astype(F32))
+                    for p in range(3)
                 )
+                shared = v0[rows[0] - SHARED :] + v1[:SHARED]
+                adjoint.append(jnp.concatenate([v0[: rows[0] - SHARED], shared, v1[SHARED:], v2], axis=0))
             both_h, both_l = split(jnp.concatenate(adjoint, axis=1))
             spread = dot(corr_h, both_h) + (dot(corr_h, both_l) + dot(corr_l, both_h))
             for u in range(2):
@@ -574,10 +572,10 @@
                 pltpu.SMEM((tiles, owners), I32),
                 dma(3), dma(2 * n + n * n), dma(2 * n + n * n), dma(4),
                 dma(6 * n), dma(6 * n),
-                dma(3 * n * n), dma(3 * n * n),
+                dma(6 * n * n), dma(6 * n * n),
                 dma(6 * n * n), dma(6 * n * n), dma(3 * n),
                 dma(6 * n * n), dma(6 * n * n), dma(3 * n),
-                dma(3 * n * n), dma(3 * n * n),
+                dma(6 * n * n), dma(6 * n * n),
                 dma(6 * n), dma(6 * n),
                 dma(2), pltpu.SemaphoreType.REGULAR,
             ]

time: 195 us -> 190 us (0.974)
  Pallas kernels: 192 us -> 187 us
    pallas_call x1, Pallas kernels: 192 us -> 187 us  [per_device(): pl.pallas_call(functools.partial(kernel, n, rows), name='gradient', out_s...]
where the time goes in v3:
time: 190 us
  Pallas kernels  187 us (98%)
  local copies, waits for them, and re-layouts  3.11 us (2%)
    pallas_call x1, Pallas kernels, per_device(): pl.pallas_call(functools.partial(kernel, n, rows), name='gradient', out_s...  187 us

profile of v3, /device:TPU:1, one launch (start us, length us, event | category | flops | bytes accessed | tf_op | source)
XLA Modules:
  0.0 190.0 jit_solution(2713013429529642580)
XLA Ops:
  0.0 186.8 %gradient.1 = f32[16,256,128]{2,1,0:T(8,128)} custom-call(s32[4,24]{1,0:T(4,128)} %ids_ref.1, f32[16,256]{1,0:T(8,128)} %prior_ref.1, f32[256,256]{1,0:T(8,128)} %corr_ref.1, f32[8,128]{1,0:T(8,128)} %bitcast.3, f32[16,256,128]{2,1,0:T(8,128)} %control_hbm.1, bf16[96,256,256]{2,1,0:T(8,128)(2,1)} %bitcast.2, f32[1024,128]{1,0:T(8,128)} %obs_hbm.1), custom_call_target="tpu_custom_call" | custom-call | tf_op jit(solution)/shard_map/gradient/pallas_call | solution.py:541
  186.8 3.1 %copy.9 = f32[16,256,128]{2,1,0:T(8,128)} copy(f32[16,256,128]{2,1,0:T(8,128)} %gradient.1) | data formatting | bytes 4194304

commit v4 on v3

--- a/solution.py
+++ b/solution.py
@@ -103,7 +103,7 @@
     out_hbm,
     g00, g01, g02, g03, g10, g11, g12, g13, g20, g21, g22, g23,
     s0, s1, s2, b0, b1, b2, a0, a1, a2, h0, h1, h2, r0, r1, r2, m0, m1, m2, o0, o1, o2,
-    foot, control, obs, out, mismatch, mine, row_ids, table, table_t, pair_v, prev_v, last_v,
+    foot, control, obs, out, weights, mismatch, mine, row_ids, table, table_t, pair_v, prev_v, last_v,
     table_s, pair_s, prev_s, last_s,
     load_sem, id_send, id_recv, scalar_sem, one_send, one_recv, two_send, two_recv, three_send, three_recv, keep_sem,
     back_three_send, back_three_recv, back_keep_sem, back_two_send, back_two_recv, back_one_send, back_one_recv,
@@ -326,6 +326,11 @@
     for p in range(3):
         chain[p][none] = jnp.zeros((rows[p], members), F32)
 
+    per = per_block // members
+    for b in range(blocks):
+        for v in range(per):
+            weights[b, v * members : (v + 1) * members] = column(weight_ref[b * per + v : b * per + v + 1, :])
+
     load_foot.wait()
     load_obs.wait()
     for copy in to_scalar + kept:
@@ -338,8 +343,6 @@
     for target in line_partners(n, xyz, core):
         pl.semaphore_signal(free_sem, inc=1, device_id=target, device_id_type=MESH)
         freed += 1
-
-    per = per_block // members
 
     def model(b, carry):
         feet, flux = [], []
@@ -356,8 +359,7 @@
             flux += [v0[: rows[0] - SHARED], shared, v1[SHARED:], v2]
             feet.append(foot[b * touched + k])
         modeled = dot(jnp.concatenate(feet, axis=1), jnp.concatenate(flux, axis=0))
-        weight = jnp.concatenate([column(weight_ref[pl.ds(b * per + v, 1), :]) for v in range(per)], axis=0)
-        wrong = (modeled - obs[pl.ds(pl.multiple_of(b * per_block, per_block), per_block), :]) * weight
+        wrong = (modeled - obs[pl.ds(pl.multiple_of(b * per_block, per_block), per_block), :]) * weights[b]
         mismatch[b] = wrong.T.astype(BF)
         return carry
 
@@ -365,6 +367,24 @@
 
     sent = []
     one_way = {}
+
+    def give_back(turn, ds, other):
+        for p, (first, second, third) in enumerate(ORDERS):
+            goal = moved(n, xyz, third, ds)
+            at_rows = sent_rows(rows, p, other)
+            lies = (turn - ds) % n
+            src = arrived[p].at[other * n + goal[third], lies, :, at_rows]
+            dst = middle[p].at[other * n + xyz[third], lies, :, at_rows]
+            if ds or other:
+                i = ((p * n + turn) * n + ds) * 2 + other
+                copy = remote(src, dst, back_three_send.at[i], back_three_recv.at[i],
+                              device_of(n, goal, lax.rem(core + other, 2)))
+                sent.append(copy)
+            else:
+                copy = pltpu.make_async_copy(src, dst, back_keep_sem.at[p * n + turn])
+                copy.start()
+            one_way.setdefault((p, lies), []).append((copy, bool(ds or other)))
+
     for turn in range(n):
 
         for other in range(2):
@@ -385,32 +405,28 @@
             if turn == 0 and other == 0:
                 pl.semaphore_wait(free_sem, freed)
             for ds in STEPS + (0,):
-                for p, (first, second, third) in enumerate(ORDERS):
-                    goal = moved(n, xyz, third, ds)
-                    at_rows = sent_rows(rows, p, other)
-                    lies = (turn - ds) % n
-                    src = arrived[p].at[other * n + goal[third], lies, :, at_rows]
-                    dst = middle[p].at[other * n + xyz[third], lies, :, at_rows]
-                    if ds or other:
-                        i = ((p * n + turn) * n + ds) * 2 + other
-                        copy = remote(src, dst, back_three_send.at[i], back_three_recv.at[i],
-                                      device_of(n, goal, lax.rem(core + other, 2)))
-                        sent.append(copy)
+                if turn == 0 or ds == turn:
+                    give_back(turn, ds, other)
+
+    for turn in range(1, n):
+        for other in range(2):
+            for ds in STEPS + (0,):
+                if ds != turn:
+                    give_back(turn, ds, other)
+
+    def arrive(first_lies):
+        for (p, lies), copies in one_way.items():
+            if (lies == 0) == first_lies:
+                for copy, far in copies:
+                    if far:
+                        copy.wait_recv()
                     else:
-                        copy = pltpu.make_async_copy(src, dst, back_keep_sem.at[p * n + turn])
-                        copy.start()
-                    one_way.setdefault(p, []).append((copy, bool(ds or other)))
-
-    for p in range(3):
-        for copy, far in one_way[p]:
-            if far:
-                copy.wait_recv()
-            else:
-                copy.wait()
+                        copy.wait()
 
     two = {}
-    for j in BACK + (0,):
-        for k in STEPS:
+
+    def pass_on(j, steps):
+        for k in steps:
             for p, (first, second, third) in enumerate(ORDERS):
                 goal = moved(n, xyz, second, k)
                 for other in range(2):
@@ -423,6 +439,13 @@
                     )
                     sent.append(two[p, k, j, other])
 
+    arrive(True)
+    for j in BACK:
+        pass_on(j, (n - j,))
+    arrive(False)
+    for j in BACK:
+        pass_on(j, [k for k in STEPS if k != n - j])
+
     one = {}
     relayed = {}
 
@@ -435,6 +458,8 @@
         return copy
 
     for j in BACK + (0,):
+        if j == 1:
+            pass_on(0, STEPS)
         for p in (1, 2, 0):
             first, second, third = ORDERS[p]
             for k in STEPS:
@@ -558,6 +583,7 @@
                 pltpu.VMEM(control.shape, F32),
                 pltpu.VMEM(obs_values.shape, F32),
                 pltpu.VMEM(control.shape, F32),
+                pltpu.VMEM((blocks, per_block, members), F32),
                 pltpu.VMEM((blocks, members, per_block), BF),
                 pltpu.VMEM((8, owners), I32),
                 pltpu.VMEM((2 * n, 8, owners), I32),

time: 190 us -> 182 us (0.958)
  Pallas kernels: 187 us -> 178 us
    pallas_call x1, Pallas kernels: 187 us -> 178 us  [per_device(): pl.pallas_call(functools.partial(kernel, n, rows), name='gradient', out_s...]
where the time goes in v4:
time: 182 us; the launch traced here: 181 us
  Pallas kernels  178 us (98%)
  local copies, waits for them, and re-layouts  3.11 us (2%)
    pallas_call x1, Pallas kernels, per_device(): pl.pallas_call(functools.partial(kernel, n, rows), name='gradient', out_s...  178 us

profile of v4, /device:TPU:1, one launch (start us, length us, event | category | flops | bytes accessed | tf_op | source)
XLA Modules:
  0.0 181.4 jit_solution(641159377506243878)
XLA Ops:
  0.0 178.3 %gradient.1 = f32[16,256,128]{2,1,0:T(8,128)} custom-call(s32[4,24]{1,0:T(4,128)} %ids_ref.1, f32[16,256]{1,0:T(8,128)} %prior_ref.1, f32[256,256]{1,0:T(8,128)} %corr_ref.1, f32[8,128]{1,0:T(8,128)} %bitcast.3, f32[16,256,128]{2,1,0:T(8,128)} %control_hbm.1, bf16[96,256,256]{2,1,0:T(8,128)(2,1)} %bitcast.2, f32[1024,128]{1,0:T(8,128)} %obs_hbm.1), custom_call_target="tpu_custom_call" | custom-call | tf_op jit(solution)/shard_map/gradient/pallas_call | solution.py:566
  178.3 3.1 %copy.9 = f32[16,256,128]{2,1,0:T(8,128)} copy(f32[16,256,128]{2,1,0:T(8,128)} %gradient.1) | data formatting | bytes 4194304

commit v5 on v4

--- a/solution.py
+++ b/solution.py
@@ -288,8 +288,6 @@
                     else:
                         kept.append(pltpu.make_async_copy(src, dst, keep_sem.at[p * n + k]))
                         kept[-1].start()
-    sent += final
-
     table_t[...] = table[...].reshape(lanes, lanes).T
     shape = (lanes, lanes)
     coords = []
@@ -335,10 +333,14 @@
     load_obs.wait()
     for copy in to_scalar + kept:
         copy.wait()
-    for copy in final:
-        copy.wait_recv()
     for copy in sent:
         copy.wait_send()
+    per_step = len(final) // n
+    for k in range(n):
+        for copy in final[k * per_step : (k + 1) * per_step]:
+            copy.wait_recv()
+        for copy in final[k * per_step : (k + 1) * per_step]:
+            copy.wait_send()
     freed = 0
     for target in line_partners(n, xyz, core):
         pl.semaphore_signal(free_sem, inc=1, device_id=target, device_id_type=MESH)
@@ -363,7 +365,7 @@
         mismatch[b] = wrong.T.astype(BF)
         return carry
 
-    lax.fori_loop(0, blocks, model, 0)
+    lax.fori_loop(0, blocks, model, 0, unroll=2)
 
     sent = []
     one_way = {}
@@ -401,7 +403,7 @@
                     )
                 return carry
 
-            lax.fori_loop(0, n * n, make, 0, unroll=4)
+            lax.fori_loop(0, n * n, make, 0, unroll=8)
             if turn == 0 and other == 0:
                 pl.semaphore_wait(free_sem, freed)
             for ds in STEPS + (0,):
@@ -515,6 +517,10 @@
                     )
 
     corr_h, corr_l = split(corr_ref[...].T)
+    late = list(one.values())
+    for copy in sent:
+        if all(copy is not other for other in late):
+            copy.wait_send()
     stores = []
     for h in range(2):
         for p in (1, 2, 0):
@@ -541,7 +547,7 @@
         stores.append(pltpu.make_async_copy(out.at[halves[h]], out_hbm.at[halves[h]], out_sem.at[h]))
         stores[-1].start()
 
-    for copy in sent:
+    for copy in late:
         copy.wait_send()
     for copy in stores:
         copy.wait()

time: 182 us -> 180 us (0.989)
  no operation moved by 1% of the time
where the time goes in v5:
time: 180 us
  Pallas kernels  177 us (98%)
  local copies, waits for them, and re-layouts  3.11 us (2%)
    pallas_call x1, Pallas kernels, per_device(): pl.pallas_call(functools.partial(kernel, n, rows), name='gradient', out_s...  177 us

profile of v5, /device:TPU:1, one launch (start us, length us, event | category | flops | bytes accessed | tf_op | source)
XLA Modules:
  0.0 180.1 jit_solution(1623436252991143916)
XLA Ops:
  0.0 177.0 %gradient.1 = f32[16,256,128]{2,1,0:T(8,128)} custom-call(s32[4,24]{1,0:T(4,128)} %ids_ref.1, f32[16,256]{1,0:T(8,128)} %prior_ref.1, f32[256,256]{1,0:T(8,128)} %corr_ref.1, f32[8,128]{1,0:T(8,128)} %bitcast.3, f32[16,256,128]{2,1,0:T(8,128)} %control_hbm.1, bf16[96,256,256]{2,1,0:T(8,128)(2,1)} %bitcast.2, f32[1024,128]{1,0:T(8,128)} %obs_hbm.1), custom_call_target="tpu_custom_call" | custom-call | tf_op jit(solution)/shard_map/gradient/pallas_call | solution.py:572
  177.0 3.1 %copy.9 = f32[16,256,128]{2,1,0:T(8,128)} copy(f32[16,256,128]{2,1,0:T(8,128)} %gradient.1) | data formatting | bytes 4194304

commit v6 on v5

--- a/solution.py
+++ b/solution.py
@@ -487,7 +487,7 @@
                             chain[p][(step * n + third_at) * 2 + other, rest] = chain[p][before, rest]
                     return carry
 
-                lax.fori_loop(0, n, link, 0)
+                lax.fori_loop(0, n, link, 0, unroll=2)
 
             for h in range(2):
                 joins = (j == 1 and h == 0) or (j == 3 and h == 1)
@@ -504,7 +504,7 @@
                         own[p][h * half + t] = total
                     return carry
 
-                lax.fori_loop(0, half, collect, 0)
+                lax.fori_loop(0, half, collect, 0, unroll=4)
                 if j == 2:
                     k = 1 if h == 0 else 3
                     relayed[p, h] = give(
@@ -543,7 +543,7 @@
                 out[t + u] = control[t + u] + spread[:, members * u : members * (u + 1)]
             return carry
 
-        lax.fori_loop(0, half // 2, finish, 0)
+        lax.fori_loop(0, half // 2, finish, 0, unroll=2)
         stores.append(pltpu.make_async_copy(out.at[halves[h]], out_hbm.at[halves[h]], out_sem.at[h]))
         stores[-1].start()
 

time: 180 us -> 180 us (level)
  no operation moved by 1% of the time
where the time goes in v6:
time: 180 us
  Pallas kernels  177 us (98%)
  local copies, waits for them, and re-layouts  3.11 us (2%)
    pallas_call x1, Pallas kernels, per_device(): pl.pallas_call(functools.partial(kernel, n, rows), name='gradient', out_s...  177 us

profile of v6, /device:TPU:1, one launch (start us, length us, event | category | flops | bytes accessed | tf_op | source)
XLA Modules:
  0.0 179.7 jit_solution(8529380967050568177)
XLA Ops:
  0.0 176.6 %gradient.1 = f32[16,256,128]{2,1,0:T(8,128)} custom-call(s32[4,24]{1,0:T(4,128)} %ids_ref.1, f32[16,256]{1,0:T(8,128)} %prior_ref.1, f32[256,256]{1,0:T(8,128)} %corr_ref.1, f32[8,128]{1,0:T(8,128)} %bitcast.3, f32[16,256,128]{2,1,0:T(8,128)} %control_hbm.1, bf16[96,256,256]{2,1,0:T(8,128)(2,1)} %bitcast.2, f32[1024,128]{1,0:T(8,128)} %obs_hbm.1), custom_call_target="tpu_custom_call" | custom-call | tf_op jit(solution)/shard_map/gradient/pallas_call | solution.py:572
  176.6 3.1 %copy.9 = f32[16,256,128]{2,1,0:T(8,128)} copy(f32[16,256,128]{2,1,0:T(8,128)} %gradient.1) | data formatting | bytes 4194304
